TPU v7x, 32 devices: a whole 2x2x4 slice. The times are simulated.
32 devices in a mesh: feat: 4 (over z), trainer: 8 (over y, x, core).
Axes of the slice: x: 2, y: 2, z: 4, core: 2. Of those that a mesh axis runs over, the one named last changes fastest.
Arguments:
- features: bfloat16 [128, 32768], P('feat', 'trainer'), may hold values from -6 to 6
- first_adjacent: int32 [4096, 15], P('trainer'), may hold values from 0 to 4095
- first_center: int32 [4096], P('trainer'), may hold values from 0 to 4095
- first_count: int32 [4096], P('trainer'), may hold values from 1 to 15
- owner_map: int32 [4096], P('trainer'), may hold values from 0 to 31, as said below
- first_root: bfloat16 [128, 1024], P('feat'), may hold values from -0.5 to 0.5
- first_near: bfloat16 [128, 1024], P('feat'), may hold values from -0.5 to 0.5
- first_bias: float32 [1024], replicated, may hold values from -3 to 3
- second_adjacent: int32 [16384, 10], P(('feat', 'trainer')), may hold values from 0 to 255, as said below
- second_center: int32 [16384], P(('feat', 'trainer')), may hold values from 0 to 255, as said below
- second_count: int32 [16384], P(('feat', 'trainer')), may hold values from 1 to 10
- second_root: bfloat16 [1024, 1024], replicated, may hold values from -0.1875 to 0.1875
- second_near: bfloat16 [1024, 1024], replicated, may hold values from -0.1875 to 0.1875
- second_bias: float32 [1024], replicated, may hold values from -3 to 3
- upstream: bfloat16 [16384, 1024], P(('feat', 'trainer')), may hold values from -0.046875 to 0.046875
Outputs:
- layer_output: bfloat16 [16384, 1024], P(('feat', 'trainer'))
- rootgrad_two: float32 [1024, 1024], replicated
- neargrad_two: float32 [1024, 1024], replicated
- biasgrad_two: float32 [1024], replicated
- rootgrad_one: float32 [128, 1024], P('feat')
- neargrad_one: float32 [128, 1024], P('feat')
- biasgrad_one: float32 [1024], replicated
Inputs may be any that keep to these rules, and one draw needn't show every extreme that they name: `owner_map`: among the 512 layer-one nodes of one trainer block at most 32 name any one owner; in every draw some owner is named by exactly 32 nodes of every block, and every owner is named by some node. `second_adjacent`: every entry names a filled row of the owner's table: row s * 32 + c with c smaller than the number of nodes of block s that name this owner. `second_center`: every entry names a filled row of the owner's table, as for second_adjacent.
All inputs are finite; a program needn't handle non-finite values.
Results may differ from a plain program's by a relative error of at most 0.025.
Values may be sent and summed in bfloat16 or wider, within the bound.
A program may use at most 128 MiB of HBM per device.

v0:
```python
import jax
import jax.numpy as jnp
from jax import lax
from jax.sharding import PartitionSpec as P

CAP = 32


def cross_rows(left, right):
    return lax.dot_general(
        left, right, (((0,), (0,)), ((), ())), preferred_element_type=jnp.float32
    )


def cross_cols(left, right):
    return lax.dot_general(
        left, right, (((1,), (1,)), ((), ())), preferred_element_type=jnp.float32
    )


def local(
    features,
    first_adjacent,
    first_center,
    first_count,
    owner_map,
    first_root,
    first_near,
    first_bias,
    second_adjacent,
    second_center,
    second_count,
    second_root,
    second_near,
    second_bias,
    upstream,
):
    feat_size = lax.axis_size("feat")
    trainers = lax.axis_size("trainer")
    owners_all = feat_size * trainers
    node_count = owner_map.shape[0]
    hidden_width = first_root.shape[1]
    block_width = features.shape[0]
    input_count = features.shape[1]
    fanout = first_adjacent.shape[1]
    slot_total = owners_all * CAP
    slots = trainers * CAP
    onehot = (owner_map[:, None] == jnp.arange(owners_all, dtype=jnp.int32)[None, :]).astype(
        jnp.int32
    )
    slot_rank = jnp.sum((jnp.cumsum(onehot, axis=0) - onehot) * onehot, axis=1)
    slot_node = (
        jnp.full((slot_total,), node_count, jnp.int32)
        .at[owner_map * CAP + slot_rank]
        .set(jnp.arange(node_count, dtype=jnp.int32))
    )
    filled = slot_node < node_count
    slot_adjacent = jnp.take(first_adjacent, slot_node, axis=0, mode="clip")
    slot_own = jnp.take(first_center, slot_node, axis=0, mode="clip")
    slot_count = jnp.where(filled, jnp.take(first_count, slot_node, axis=0, mode="clip"), 1)
    block_size = 512
    block_total = slot_total // block_size
    input_ids = jnp.arange(input_count, dtype=jnp.int32)[:, None]

    def select_block(pieces):
        adjacent_block, own_block, count_block, filled_block = pieces
        multiples = jnp.zeros((input_count, block_size), jnp.float32)
        for column in range(fanout):
            hits = (input_ids == adjacent_block[None, :, column]) & (
                (column < count_block) & filled_block
            )[None, :]
            multiples = multiples + jnp.where(hits, jnp.float32(1.0), jnp.float32(0.0))
        own_pick = ((input_ids == own_block[None, :]) & filled_block[None, :]).astype(jnp.bfloat16)
        own_cols = jnp.dot(features, own_pick, preferred_element_type=jnp.float32).astype(
            jnp.bfloat16
        )
        near_sum = jnp.dot(
            features, multiples.astype(jnp.bfloat16), preferred_element_type=jnp.float32
        )
        near_cols = (near_sum / count_block.astype(jnp.float32)[None, :]).astype(jnp.bfloat16)
        return (own_cols, near_cols)

    blocks_in = (
        slot_adjacent.reshape(block_total, block_size, fanout),
        slot_own.reshape(block_total, block_size),
        slot_count.reshape(block_total, block_size),
        filled.reshape(block_total, block_size),
    )
    own_blocks, near_blocks = lax.map(select_block, blocks_in)
    slot_center = own_blocks.transpose(1, 0, 2).reshape(block_width, slot_total)
    slot_near = near_blocks.transpose(1, 0, 2).reshape(block_width, slot_total)
    packed = jnp.stack([slot_center, slot_near]).reshape(2, block_width, owners_all, CAP)
    arrived = lax.all_to_all(packed, ("feat", "trainer"), split_axis=2, concat_axis=2, tiled=True)
    arrived = (
        arrived.reshape(2, block_width, feat_size, trainers, CAP)
        .transpose(0, 2, 1, 3, 4)
        .reshape(2, feat_size * block_width, slots)
    )
    owner_center = arrived[0]
    owner_near = arrived[1]
    root_all, near_all = (
        lax.all_gather(first_root, "feat", axis=0, tiled=True),
        lax.all_gather(first_near, "feat", axis=0, tiled=True),
    )
    pre_one = jnp.zeros((slots, hidden_width), jnp.float32) + first_bias
    for quarter in range(feat_size):
        low = quarter * block_width
        high = low + block_width
        part = cross_rows(owner_center[low:high], root_all[low:high]) + cross_rows(
            owner_near[low:high], near_all[low:high]
        )
        pre_one = pre_one + part.astype(jnp.bfloat16).astype(jnp.float32)
    hidden_table = jax.nn.softplus(pre_one).astype(jnp.bfloat16)
    slot_ids = jnp.arange(slots, dtype=jnp.int32)
    root_pick = (second_center[:, None] == slot_ids[None, :]).astype(jnp.bfloat16)
    root_rows = jnp.dot(root_pick, hidden_table, preferred_element_type=jnp.float32).astype(
        jnp.bfloat16
    )
    multiples = jnp.zeros((second_center.shape[0], slots), jnp.float32)
    for column in range(second_adjacent.shape[1]):
        hits = (column < second_count)[:, None] & (
            second_adjacent[:, column : column + 1] == slot_ids[None, :]
        )
        multiples = multiples + jnp.where(hits, jnp.float32(1.0), jnp.float32(0.0))
    multiples = multiples.astype(jnp.bfloat16)
    divisor = second_count.astype(jnp.float32)[:, None]
    near_two = (
        jnp.dot(multiples, hidden_table, preferred_element_type=jnp.float32) / divisor
    ).astype(jnp.bfloat16)
    pre_two = jnp.dot(root_rows, second_root, preferred_element_type=jnp.float32)
    pre_two = (
        pre_two + jnp.dot(near_two, second_near, preferred_element_type=jnp.float32) + second_bias
    )
    gate = jax.nn.sigmoid(pre_two)
    layer_output = (pre_two * gate).astype(jnp.bfloat16)
    slope_two = (upstream.astype(jnp.float32) * gate * (1.0 + pre_two * (1.0 - gate))).astype(
        jnp.bfloat16
    )
    rootgrad_two, neargrad_two, biasgrad_two = lax.psum(
        (
            cross_rows(root_rows, slope_two),
            cross_rows(near_two, slope_two),
            jnp.sum(slope_two.astype(jnp.float32), axis=0),
        ),
        ("feat", "trainer"),
    )
    back_root = cross_cols(slope_two, second_root).astype(jnp.bfloat16)
    back_near = (cross_cols(slope_two, second_near) / divisor).astype(jnp.bfloat16)
    table_grad = cross_rows(root_pick, back_root) + cross_rows(multiples, back_near)
    pre_grad = (table_grad * (1.0 - jnp.exp(-hidden_table.astype(jnp.float32)))).astype(
        jnp.bfloat16
    )
    root_full = jnp.dot(owner_center, pre_grad, preferred_element_type=jnp.float32)
    near_full = jnp.dot(owner_near, pre_grad, preferred_element_type=jnp.float32)
    bias_full = jnp.sum(pre_grad.astype(jnp.float32), axis=0)
    root_sum, near_sum, biasgrad_one = lax.psum(
        (root_full, near_full, bias_full), ("feat", "trainer")
    )
    offset = lax.axis_index("feat") * block_width
    rootgrad_one = lax.dynamic_slice_in_dim(root_sum, offset, block_width, 0)
    neargrad_one = lax.dynamic_slice_in_dim(near_sum, offset, block_width, 0)
    return (
        layer_output,
        rootgrad_two,
        neargrad_two,
        biasgrad_two,
        rootgrad_one,
        neargrad_one,
        biasgrad_one,
    )


def solution(mesh):
    return jax.shard_map(
        local,
        mesh=mesh,
        in_specs=(
            P("feat", "trainer"),
            P("trainer", None),
            P("trainer"),
            P("trainer"),
            P("trainer"),
            P("feat", None),
            P("feat", None),
            P(),
            P(("feat", "trainer"), None),
            P(("feat", "trainer")),
            P(("feat", "trainer")),
            P(),
            P(),
            P(),
            P(("feat", "trainer"), None),
        ),
        out_specs=(
            P(("feat", "trainer"), None),
            P(),
            P(),
            P(),
            P("feat", None),
            P("feat", None),
            P(),
        ),
        check_vma=False,
    )
```

profile of v0, /device:TPU:0, one launch (start us, length us, event | category | flops | bytes accessed | tf_op | source)
XLA Modules:
  0.0 387.0 jit_solution(12324662637474530133)
XLA Ops:
  7.2 0.8 fusion.97
  8.0 1.2 reduce-window.6
  9.5 0.8 fusion.84
  10.3 0.7 compare_select_fusion.1
  10.9 2.4 scatter_custom_fusion
  13.4 6.9 %gather_fusion.2 = s32[1024]{0:T(1024)S(1)} fusion(s32[512]{0:T(512)S(1)} %copy-done.1, s32[1024]{0:T(1024)S(1)} %broadcast_clamp_fusion), kind=kCustom, calls=%fused_computation.2 | custom fusion | bytes 12288 | tf_op jit(solution)/shard_map/jit(_take)/gather | solution.py:60
  20.5 2.8 gather_fusion.1
  23.5 6.9 %gather_fusion = s32[1024]{0:T(1024)S(1)} fusion(s32[512]{0:T(512)S(1)} %copy-done.2, s32[1024]{0:T(1024)S(1)} %broadcast_clamp_fusion), kind=kCustom, calls=%fused_computation | custom fusion | bytes 12288 | tf_op jit(solution)/shard_map/jit(_take)/gather | solution.py:59
  30.4 58.3 %while.14 = (s32[]{:T(128)}, bf16[2,32,512]{2,1,0:T(8,128)(2,1)S(1)}, bf16[2,32,512]{2,1,0:T(8,128)(2,1)S(1)}, s32[2,512]{1,0:T(2,128)S(1)}, pred[2,512]{1,0:T(4...) while((s32[]{:T(128)}, ...), condition=%wide.region_5.6_spmd.clone.clone, body=%wide.region_4.5_spmd.clone.clone.sunk | while | flops 398523904 | bytes 776817 | solution.py:89
  30.8 27.1 %fusion.151 = bf16[2,32,512]{2,1,0:T(8,128)(2,1)S(1)} fusion(bf16[2,32,512]{2,1,0:T(8,128)(2,1)S(1)} %get-tuple-element.403, s32[]{:T(128)} %get-tuple-element.401, bf16[32,4096]{1,0:T(8,128)(2,1)S(1)} %get-tuple-element.415, s32[512]{0:T(512)S(1)} %bitcast.172, s32[512]{0:T(512)S(1)} %bitcast.173, s32[512]{0:T(512)S(1)} %bitcast.174, ...), kind=kOutput, calls=%fused_computation.63.clone.1 | convolution fusion | flops 260079616 | bytes 335364 | tf_op jit(solution)/shard_map/while/body/eval_jaxpr/dot_general | solution.py:77
  57.9 1.7 fusion.149
  59.8 27.1 %fusion.151 = bf16[2,32,512]{2,1,0:T(8,128)(2,1)S(1)} fusion(bf16[2,32,512]{2,1,0:T(8,128)(2,1)S(1)} %get-tuple-element.403, s32[]{:T(128)} %get-tuple-element.401, bf16[32,4096]{1,0:T(8,128)(2,1)S(1)} %get-tuple-element.415, s32[512]{0:T(512)S(1)} %bitcast.172, s32[512]{0:T(512)S(1)} %bitcast.173, s32[512]{0:T(512)S(1)} %bitcast.174, ...), kind=kOutput, calls=%fused_computation.63.clone.1 | convolution fusion | flops 260079616 | bytes 335364 | tf_op jit(solution)/shard_map/while/body/eval_jaxpr/dot_general | solution.py:77
  86.9 1.7 fusion.149
  89.7 1.2 reshape.153
  90.9 7.3 %all-to-all-start = ((bf16[32,2,1024]{2,1,0:T(2,128)(2,1)}), bf16[32,2,1024]{2,1,0:T(2,128)(2,1)S(1)}, u32[]{:S(2)}, u32[]{:S(2)}) async-start(bf16[32,2,1024]{2,1,0:T(2,128)(2,1)} %reshape.153), calls=%async_computation | async-start | bytes 262144 | tf_op jit(solution)/shard_map/all_to_all | solution.py:93
  98.3 15.2 %all_gather.6 = bf16[128,1024]{1,0:T(8,128)(2,1)S(1)} all-gather(bf16[32,1024]{1,0:T(8,128)(2,1)S(1)} %copy-done.14), channel_id=1, replica_groups=mesh['feat'=4,'trainer'=8] {'feat'}, dimensions={0}, use_global_device_ids=true | all-gather | bytes 327680 | tf_op jit(solution)/shard_map/all_gather | solution.py:102
  113.5 0.6 broadcast_compare_fusion.10
  114.1 15.1 %all_gather.7 = bf16[128,1024]{1,0:T(8,128)(2,1)} all-gather(bf16[32,1024]{1,0:T(8,128)(2,1)S(1)} %copy-done.15), channel_id=1, replica_groups=mesh['feat'=4,'trainer'=8] {'feat'}, dimensions={0}, use_global_device_ids=true | all-gather | bytes 327680 | tf_op jit(solution)/shard_map/all_gather | solution.py:103
  129.8 0.6 fusion.104
  131.0 0.7 fusion.103
  131.7 0.8 fusion.102
  132.8 0.7 slice.178
  133.5 1.3 fusion.95
  134.8 1.0 fusion.92
  135.8 1.6 slice.181
  137.4 1.6 slice.184
  138.9 2.0 fusion.89
  140.9 1.6 slice.187
  142.5 0.7 slice.190
  143.2 2.0 fusion.86
  145.4 1.5 fusion.66
  147.3 0.9 copy-done.3
  148.5 0.9 copy-done.7
  149.4 0.8 fusion.68
  151.2 1.3 fusion.105
  152.7 3.4 divide_convert_fusion.1
  156.1 3.5 convert_reduce_fusion
  159.6 4.4 %fusion.67 = f32[256,1024]{1,0:T(8,128)} fusion(bf16[512,1024]{1,0:T(8,128)(2,1)} %get-tuple-element.221, bf16[1024,1024]{1,0:T(8,128)(2,1)S(1)} %copy-done, f32[512]{0:T(512)S(1)} %copy-done.30, s32[512]{0:T(512)S(1)} %bitcast.206, s32[512]{0:T(512)S(1)} %bitcast.208, s32[512]{0:T(512)S(1)} %bitcast.192, s32[512]{0:T(512)S(1)} %bitcast.194, ...), kind=kOutput, calls=%fused_computation.114 | convolution fusion | flops 1348468736 | bytes 4221952 | tf_op jit(solution)/shard_map/dot_general | solution.py:10
  164.0 4.9 %fusion.107 = f32[1024,1024]{1,0:T(8,128)} fusion(bf16[512,1024]{1,0:T(8,128)(2,1)} %copy-done.6, bf16[512,1024]{1,0:T(8,128)(2,1)} %get-tuple-element.221), kind=kOutput, calls=%fused_computation.191 | convolution fusion | flops 1073741824 | bytes 6291456 | tf_op jit(solution)/shard_map/dot_general | solution.py:10
  169.0 3.3 fusion.106
  172.3 4.0 %convert_reduce_fusion.1 = (f32[1024]{0:T(1024)S(1)}, bf16[256,1024]{1,0:T(8,128)(2,1)S(1)}) fusion(bf16[256,1024]{1,0:T(8,128)(2,1)} %copy-done.11, f32[256,1024]{1,0:T(8,128)} %fusion.67, bf16[512,1024]{1,0:T(8,128)(2,1)} %get-tuple-element.221, bf16[1024,1024]{1,0:T(8,128)(2,1)} %param.28, s32[512]{0:T(512)S(1)} %copy-done.19), kind=kOutput, calls=%fused_computation.116 | convolution fusion | flops 1344928768 | bytes 5249024 | tf_op jit(solution)/shard_map/dot_general | solution.py:10
  176.7 1.0 fusion.109
  177.7 1.0 fusion.108
  178.8 40.5 %all-reduce = (f32[1024]{0:T(1024)}, f32[1024]{0:T(1024)}) all-reduce(f32[1024]{0:T(1024)S(1)} %get-tuple-element.220, f32[1024]{0:T(1024)S(1)} %get-tuple-element.271), channel_id=1, replica_groups=mesh['feat'=4,'trainer'=8] {'feat','trainer'}, use_global_device_ids=true, to_apply=%region_9.10 | all-reduce | flops 2048 | bytes 16384 | tf_op jit(solution)/shard_map/psum | solution.py:139
  219.2 152.3 %all-reduce.4.cloned.1.call-done = (f32[1024,1024]{1,0:T(8,128)}, f32[1024,1024]{1,0:T(8,128)}, f32[128,1024]{1,0:T(8,128)}, f32[128,1024]{1,0:T(8,128)}) async-done(((f32[1024,1024]{1,0:T(8,128)}, f32[1024,1024]{1,0:T(8,128)}, f32[128,1024]{1,0:T(8,128)}, f32[128,1024]{1,0:T(8,128)}), (f32[1024,1024]{1,0:T(8,128)}, f32[1024,1024]{1,0:T(8,128)}, f32[128,1024]{1,0:T(8,128)}, ...) | async-done | bytes 9437200 | tf_op jit(solution)/shard_map/psum | solution.py:139
  371.5 1.7 constant_dynamic-slice_fusion.3
  373.2 4.9 %copy.58 = f32[1024,1024]{1,0:T(8,128)} copy(f32[1024,1024]{1,0:T(8,128)} %get-tuple-element.420) | data formatting | bytes 8388608
  378.2 2.0 copy.59
  (129 shorter events, 5.3 us)
Async XLA Ops:
  7.2 148.9 %copy-start = (bf16[1024,1024]{1,0:T(8,128)(2,1)S(1)}, bf16[1024,1024]{1,0:T(8,128)(2,1)}, u32[]{:S(2)}) copy-start(bf16[1024,1024]{1,0:T(8,128)(2,1)} %param.29) | copy-start | bytes 6291460
  7.2 6.2 %copy-start.1 = (s32[512]{0:T(512)S(1)}, s32[512]{0:T(512)}, u32[]{:S(2)}) copy-start(s32[512]{0:T(512)} %param.20) | copy-start | bytes 6148
  13.4 6.9 %copy-start.16 = (s32[512,15]{0,1:T(8,128)S(1)}, s32[512,15]{0,1:T(8,128)}, u32[]{:S(2)}) copy-start(s32[512,15]{0,1:T(8,128)} %param.18) | copy-start | bytes 92164
  20.5 3.0 copy-start.2
  23.5 6.9 %copy-start.43 = (bf16[32,4096]{1,0:T(8,128)(2,1)S(1)}, bf16[32,4096]{1,0:T(8,128)(2,1)}, u32[]{:S(2)}) copy-start(bf16[32,4096]{1,0:T(8,128)(2,1)} %param.17) | copy-start | bytes 786436
  88.8 9.5 %copy-start.14 = (bf16[32,1024]{1,0:T(8,128)(2,1)S(1)}, bf16[32,1024]{1,0:T(8,128)(2,1)}, u32[]{:S(2)}) copy-start(bf16[32,1024]{1,0:T(8,128)(2,1)} %param.22) | copy-start | bytes 196612
  88.9 24.6 %copy-start.18 = (s32[512]{0:T(512)S(1)}, s32[512]{0:T(512)}, u32[]{:S(2)}) copy-start(s32[512]{0:T(512)} %param.27) | copy-start | bytes 6148
  88.9 25.2 %copy-start.15 = (bf16[32,1024]{1,0:T(8,128)(2,1)S(1)}, bf16[32,1024]{1,0:T(8,128)(2,1)}, u32[]{:S(2)}) copy-start(bf16[32,1024]{1,0:T(8,128)(2,1)} %param.23) | copy-start | bytes 196612
  89.1 40.7 %copy-start.17 = (s32[512,10]{0,1:T(8,128)S(1)}, s32[512,10]{0,1:T(8,128)}, u32[]{:S(2)}) copy-start(s32[512,10]{0,1:T(8,128)} %param.25) | copy-start | bytes 61444
  90.9 39.5 %all-to-all-start = ((bf16[32,2,1024]{2,1,0:T(2,128)(2,1)}), bf16[32,2,1024]{2,1,0:T(2,128)(2,1)S(1)}, u32[]{:S(2)}, u32[]{:S(2)}) async-start(bf16[32,2,1024]{2,1,0:T(2,128)(2,1)} %reshape.153), calls=%async_computation | async-start | bytes 262144 | tf_op jit(solution)/shard_map/all_to_all | solution.py:93
  98.2 273.3 %all-reduce.4.cloned.1.call-start = ((), (), s32[]{:S(2)}) async-start(), calls=%async_computation.1 | async-start | bytes 18874368 | tf_op jit(solution)/shard_map/psum | solution.py:139
  143.2 3.7 copy-start.12
  145.2 1.7 copy-start.10
  146.9 1.2 copy-start.3
  146.9 1.2 copy-start.13
  148.1 1.2 copy-start.7
  149.4 0.8 copy-start.19
  149.4 1.6 copy-start.41
  150.2 2.2 copy-start.11
  151.0 1.5 copy-start.20
  151.0 1.5 copy-start.21
  151.0 1.5 copy-start.22
  151.0 1.5 copy-start.23
  151.0 1.5 copy-start.24
  151.0 1.5 copy-start.25
  151.0 1.5 copy-start.26
  151.0 1.5 copy-start.27
  151.0 1.5 copy-start.28
  151.0 1.5 copy-start.29
  151.1 1.5 copy-start.30
  151.1 1.5 copy-start.31
  151.1 1.5 copy-start.32
  151.1 1.5 copy-start.33
  151.1 1.5 copy-start.34
  151.1 1.5 copy-start.35
  151.1 1.5 copy-start.36
  151.1 1.5 copy-start.37
  151.1 1.5 copy-start.38
  151.1 1.5 copy-start.39
  151.2 1.5 copy-start.40
  152.6 3.4 copy-start.42
  152.7 3.4 copy-start.44
  156.1 3.5 copy-start.6
  164.0 4.9 %copy-start.5 = (bf16[512,1024]{1,0:T(8,128)(2,1)S(1)}, bf16[512,1024]{1,0:T(8,128)(2,1)}, u32[]{:S(2)}) copy-start(bf16[512,1024]{1,0:T(8,128)(2,1)} %get-tuple-element.221) | copy-start | bytes 3145732
  172.3 4.0 %copy-start.9 = (bf16[1,4,32,8,32]{4,3,2,1,0:T(8,128)(2,1)S(1)}, bf16[1,4,32,8,32]{4,3,2,1,0:T(8,128)(2,1)}, u32[]{:S(2)}) copy-start(bf16[1,4,32,8,32]{4,3,2,1,0:T(8,128)(2,1)} %get-tuple-element.241) | copy-start | bytes 196612
  172.3 4.2 %copy-start.8 = (bf16[1,4,32,8,32]{4,3,2,1,0:T(8,128)(2,1)S(1)}, bf16[1,4,32,8,32]{4,3,2,1,0:T(8,128)(2,1)}, u32[]{:S(2)}) copy-start(bf16[1,4,32,8,32]{4,3,2,1,0:T(8,128)(2,1)} %get-tuple-element.242) | copy-start | bytes 196612
  373.2 4.9 %copy-start.4 = (f32[1024,1024]{1,0:T(8,128)S(1)}, f32[1024,1024]{1,0:T(8,128)}, u32[]{:S(2)}) copy-start(f32[1024,1024]{1,0:T(8,128)} %get-tuple-element.421) | copy-start | bytes 12582916
Sparse Core Ops, SparseCore 0:
  178.9 192.5 all-reduce.3
where the time goes:
time: 388 us; the launch traced here: 387 us
  waiting for transfers between devices  152 us (39%)
  matrix products  94.2 us (24%)
  blocking collectives  70.8 us (18%)
  local copies, waits for them, and re-layouts  42 us (11%)
  between operations  14.8 us (4%)
  starting transfers between devices  7.34 us (2%)
  other arithmetic  5.1 us (1%)
    psum x1, waiting for transfers between devices, local(): lax.psum((cross_rows(root_rows, slope_two), cross_rows(near_two, slope_tw...  152 us
    dot_general x2, matrix products, select_block(): jnp.dot(features, multiples.astype(jnp.bfloat16), preferred_element_type=...  54.2 us
    psum x1, blocking collectives, local(): lax.psum((cross_rows(root_rows, slope_two), cross_rows(near_two, slope_tw...  40.5 us
    dot_general x12, matrix products, cross_rows(): lax.dot_general(left, right, (((0,), (0,)), ((), ())), preferred_element_...  26 us
    all_gather x1, blocking collectives, local(): lax.all_gather(first_root, 'feat', axis=0, tiled=True)  15.2 us
    all_gather x1, blocking collectives, local(): lax.all_gather(first_near, 'feat', axis=0, tiled=True)  15.1 us
    unnamed x96, local copies, waits for them, and re-layouts  11 us
  transfers between devices with their start and end apart: 2, of which 1 were waited for; matrix products, arithmetic and copies ran while one was open for 0% of the time, Pallas kernels for 0%

commit v1 on v0

v1 whole, which is shorter than its diff:
```python
import functools

import jax
import jax.numpy as jnp
from jax import lax
from jax.experimental import pallas as pl
from jax.experimental.pallas import tpu as pltpu
from jax.sharding import PartitionSpec as P

CAP = 32


CHUNK = 256
ROWS = 16
LANES = 128


def select_kernel(fanout, ids_ref, feat_ref, out_ref, picks):
    width, inputs = feat_ref.shape
    nodes = ids_ref.shape[1]
    out_ref[...] = jnp.zeros_like(out_ref)
    inner = (
        lax.broadcasted_iota(jnp.int32, (CHUNK // ROWS, ROWS, LANES), 0) * ROWS
        + lax.broadcasted_iota(jnp.int32, (CHUNK // ROWS, ROWS, LANES), 1)
    ).astype(jnp.float32).astype(jnp.bfloat16)
    one, zero = jnp.bfloat16(1.0), jnp.bfloat16(0.0)

    def chunk_step(chunk, carry):
        start = pl.multiple_of(chunk * CHUNK, CHUNK)
        for tile in range(nodes // LANES):
            lanes = slice(tile * LANES, (tile + 1) * LANES)
            local_ids = ids_ref[:, lanes] - start
            local_ids = jnp.where((local_ids >= 0) & (local_ids < CHUNK), local_ids, -1)
            local_ids = local_ids.astype(jnp.float32)
            total = None
            for column in range(fanout + 1):
                row = jnp.broadcast_to(local_ids[column : column + 1], (ROWS, LANES))
                hit = jnp.where(inner == row.astype(jnp.bfloat16)[None], one, zero)
                if column == fanout:
                    picks[:, nodes + tile * LANES : nodes + (tile + 1) * LANES] = hit.reshape(
                        CHUNK, LANES
                    )
                else:
                    total = hit if total is None else total + hit
            picks[:, lanes] = total.reshape(CHUNK, LANES)
        out_ref[...] += jnp.dot(
            feat_ref[:, pl.ds(start, CHUNK)], picks[...], preferred_element_type=jnp.float32
        )
        return carry

    lax.fori_loop(0, inputs // CHUNK, chunk_step, 0)


def select(features, adjacent, center, count):
    width, inputs = features.shape
    nodes, fanout = adjacent.shape
    columns = jnp.arange(fanout, dtype=jnp.int32)[None, :]
    ids = jnp.where(columns < count[:, None], adjacent, -1)
    ids = jnp.concatenate([ids, center[:, None]], axis=1).T
    block = 512
    steps = nodes // block
    out = pl.pallas_call(
        functools.partial(select_kernel, fanout),
        grid=(steps,),
        in_specs=[
            pl.BlockSpec((fanout + 1, block), lambda i: (0, i)),
            pl.BlockSpec((width, inputs), lambda i: (0, 0)),
        ],
        out_specs=pl.BlockSpec((width, 2 * block), lambda i: (0, i)),
        out_shape=jax.ShapeDtypeStruct((width, 2 * nodes), jnp.float32),
        scratch_shapes=[pltpu.VMEM((CHUNK, 2 * block), jnp.bfloat16)],
        cost_estimate=pl.CostEstimate(
            flops=40 * nodes * inputs * width, bytes_accessed=width * inputs * 2, transcendentals=0
        ),
    )(ids, features)
    out = out.reshape(width, steps, 2, block)
    return out[:, :, 1].reshape(width, nodes), out[:, :, 0].reshape(width, nodes)


def cross_rows(left, right):
    return lax.dot_general(
        left, right, (((0,), (0,)), ((), ())), preferred_element_type=jnp.float32
    )


def cross_cols(left, right):
    return lax.dot_general(
        left, right, (((1,), (1,)), ((), ())), preferred_element_type=jnp.float32
    )


def local(
    features,
    first_adjacent,
    first_center,
    first_count,
    owner_map,
    first_root,
    first_near,
    first_bias,
    second_adjacent,
    second_center,
    second_count,
    second_root,
    second_near,
    second_bias,
    upstream,
):
    feat_size = lax.axis_size("feat")
    trainers = lax.axis_size("trainer")
    owners_all = feat_size * trainers
    node_count = owner_map.shape[0]
    block_width = features.shape[0]
    slot_total = owners_all * CAP
    slots = trainers * CAP
    node_ids = jnp.arange(node_count, dtype=jnp.int32)
    earlier = (owner_map[:, None] == owner_map[None, :]) & (node_ids[:, None] < node_ids[None, :])
    slot_rank = jnp.sum(earlier.astype(jnp.int32), axis=0)
    position = owner_map * CAP + slot_rank
    own_cols, near_sum = select(features, first_adjacent, first_center, first_count)
    near_cols = (near_sum / first_count.astype(jnp.float32)[None, :]).astype(jnp.bfloat16)
    node_cols = jnp.concatenate([own_cols.astype(jnp.bfloat16), near_cols], axis=0)
    to_slot = (position[:, None] == jnp.arange(slot_total, dtype=jnp.int32)[None, :]).astype(
        jnp.bfloat16
    )
    packed = jnp.dot(node_cols, to_slot, preferred_element_type=jnp.float32).astype(jnp.bfloat16)
    packed = packed.reshape(2 * block_width, owners_all, CAP)
    arrived = lax.all_to_all(packed, ("feat", "trainer"), split_axis=1, concat_axis=1, tiled=True)
    arrived = (
        arrived.reshape(2, block_width, feat_size, trainers, CAP)
        .transpose(0, 2, 1, 3, 4)
        .reshape(2 * feat_size * block_width, slots)
    )
    root_all, near_all = (
        lax.all_gather(first_root, "feat", axis=0, tiled=True),
        lax.all_gather(first_near, "feat", axis=0, tiled=True),
    )
    pre_one = cross_rows(arrived, jnp.concatenate([root_all, near_all], axis=0)) + first_bias
    hidden_table = jax.nn.softplus(pre_one).astype(jnp.bfloat16)
    slot_ids = jnp.arange(slots, dtype=jnp.int32)
    root_pick = (second_center[:, None] == slot_ids[None, :]).astype(jnp.bfloat16)
    root_rows = jnp.dot(root_pick, hidden_table, preferred_element_type=jnp.float32).astype(
        jnp.bfloat16
    )
    multiples = jnp.zeros((second_center.shape[0], slots), jnp.float32)
    for column in range(second_adjacent.shape[1]):
        hits = (column < second_count)[:, None] & (
            second_adjacent[:, column : column + 1] == slot_ids[None, :]
        )
        multiples = multiples + jnp.where(hits, jnp.float32(1.0), jnp.float32(0.0))
    multiples = multiples.astype(jnp.bfloat16)
    divisor = second_count.astype(jnp.float32)[:, None]
    near_two = (
        jnp.dot(multiples, hidden_table, preferred_element_type=jnp.float32) / divisor
    ).astype(jnp.bfloat16)
    pre_two = jnp.dot(root_rows, second_root, preferred_element_type=jnp.float32)
    pre_two = (
        pre_two + jnp.dot(near_two, second_near, preferred_element_type=jnp.float32) + second_bias
    )
    gate = jax.nn.sigmoid(pre_two)
    layer_output = (pre_two * gate).astype(jnp.bfloat16)
    slope_two = (upstream.astype(jnp.float32) * gate * (1.0 + pre_two * (1.0 - gate))).astype(
        jnp.bfloat16
    )
    both = jnp.concatenate([root_rows, near_two], axis=1)
    grad_two = lax.psum(cross_rows(both, slope_two).astype(jnp.bfloat16), ("feat", "trainer"))
    back_root = cross_cols(slope_two, second_root).astype(jnp.bfloat16)
    back_near = (cross_cols(slope_two, second_near) / divisor).astype(jnp.bfloat16)
    table_grad = cross_rows(root_pick, back_root) + cross_rows(multiples, back_near)
    pre_grad = (table_grad * (1.0 - jnp.exp(-hidden_table.astype(jnp.float32)))).astype(
        jnp.bfloat16
    )
    grad_one = jnp.dot(arrived, pre_grad, preferred_element_type=jnp.float32)
    grad_one = grad_one.astype(jnp.bfloat16).reshape(2, feat_size, block_width, -1)
    grad_one = lax.psum(grad_one, ("feat", "trainer"))
    grad_one = lax.dynamic_index_in_dim(grad_one, lax.axis_index("feat"), 1, keepdims=False)
    biases = jnp.stack(
        [
            jnp.sum(slope_two.astype(jnp.float32), axis=0),
            jnp.sum(pre_grad.astype(jnp.float32), axis=0),
        ]
    )
    biasgrad_two, biasgrad_one = lax.psum(biases, ("feat", "trainer"))
    grad_two = grad_two.astype(jnp.float32).reshape(2, -1, grad_two.shape[1])
    rootgrad_two, neargrad_two = grad_two
    rootgrad_one, neargrad_one = grad_one.astype(jnp.float32)
    return (
        layer_output,
        rootgrad_two,
        neargrad_two,
        biasgrad_two,
        rootgrad_one,
        neargrad_one,
        biasgrad_one,
    )


def solution(mesh):
    return jax.shard_map(
        local,
        mesh=mesh,
        in_specs=(
            P("feat", "trainer"),
            P("trainer", None),
            P("trainer"),
            P("trainer"),
            P("trainer"),
            P("feat", None),
            P("feat", None),
            P(),
            P(("feat", "trainer"), None),
            P(("feat", "trainer")),
            P(("feat", "trainer")),
            P(),
            P(),
            P(),
            P(("feat", "trainer"), None),
        ),
        out_specs=(
            P(("feat", "trainer"), None),
            P(),
            P(),
            P(),
            P("feat", None),
            P("feat", None),
            P(),
        ),
        check_vma=False,
    )
```

time: 388 us -> 254 us (0.65)
  matrix products: 94.2 us -> 26.4 us
  waiting for transfers between devices: 152 us -> 105 us
  local copies, waits for them, and re-layouts: 42 us -> 12.3 us
  Pallas kernels: 0 us -> 12.4 us
    dot_general x6 -> x2, matrix products: 59.6 us -> 1.67 us  [the longest x1 1.1 us: local(): grad_one = jnp.dot(arrived, pre_grad, preferred_element_type=jnp.float32)]
    psum x1, waiting for transfers between devices: 152 us -> 105 us  [local(): lax.psum(cross_rows(both, slope_two).astype(jnp.bfloat16), ('feat', 'trai...]
    gather x3 -> x0, local copies, waits for them, and re-layouts: 16.6 us -> none  [the longest x1 6.87 us: local(): slot_own = jnp.take(first_center, slot_node, axis=0, mode='clip')]
    pallas_call x0 -> x1, Pallas kernels: none -> 12.4 us  [select(): pl.pallas_call(functools.partial(select_kernel, fanout), grid=(steps,), i...]
    dot_general x12 -> x4, matrix products: 26 us -> 16.2 us  [cross_rows(): lax.dot_general(left, right, (((0,), (0,)), ((), ())), preferred_element_...]
    unnamed x96 -> x63, local copies, waits for them, and re-layouts: 11 us -> 1.23 us
    slice x13 -> x2, local copies, waits for them, and re-layouts: 8.24 us -> 0.12 us  [the longest x1 0.07 us: select(): out[:, :, 1].reshape(width, nodes)]
    another operation x4 -> x3, local copies, waits for them, and re-layouts: 0.58 us -> 7.98 us  [the longest x1 6.66 us: local(): rootgrad_two, neargrad_two = grad_two]
  transfers between devices with their start and end apart: 2 -> 2, of which waited for: 1 -> 1; matrix products, arithmetic and copies ran while one was open for 0% -> 1% of each run, Pallas kernels for 0% -> 0%
where the time goes in v1:
time: 254 us; the launch traced here: 253 us
  waiting for transfers between devices  105 us (41%)
  blocking collectives  70 us (28%)
  matrix products  26.4 us (10%)
  between operations  14.6 us (6%)
  Pallas kernels  12.4 us (5%)
  local copies, waits for them, and re-layouts  12.3 us (5%)
  starting transfers between devices  7.34 us (3%)
  other arithmetic  5.23 us (2%)
    psum x1, waiting for transfers between devices, local(): lax.psum(cross_rows(both, slope_two).astype(jnp.bfloat16), ('feat', 'trai...  105 us
    psum x1, blocking collectives, local(): biasgrad_two, biasgrad_one = lax.psum(biases, ('feat', 'trainer'))  39.9 us
    dot_general x4, matrix products, cross_rows(): lax.dot_general(left, right, (((0,), (0,)), ((), ())), preferred_element_...  16.2 us
    all_gather x1, blocking collectives, local(): lax.all_gather(first_near, 'feat', axis=0, tiled=True)  15.4 us
    all_gather x1, blocking collectives, local(): lax.all_gather(first_root, 'feat', axis=0, tiled=True)  14.6 us
    pallas_call x1, Pallas kernels, select(): pl.pallas_call(functools.partial(select_kernel, fanout), grid=(steps,), i...  12.4 us
    all_to_all x1, starting transfers between devices, local(): lax.all_to_all(packed, ('feat', 'trainer'), split_axis=1, concat_axis=1,...  7.3 us
    another operation x1, local copies, waits for them, and re-layouts, local(): rootgrad_two, neargrad_two = grad_two  6.66 us
  transfers between devices with their start and end apart: 2, of which 1 were waited for; matrix products, arithmetic and copies ran while one was open for 1% of the time, Pallas kernels for 0%

profile of v1, /device:TPU:0, one launch (start us, length us, event | category | flops | bytes accessed | tf_op | source)
XLA Modules:
  0.0 253.3 jit_solution(6209283582039497858)
XLA Ops:
  7.2 0.0 copy-start
  7.2 0.8 convert_element_type.74
  8.0 0.8 fusion.32
  8.8 1.3 add_bitcast_fusion.ids_ref
  10.1 12.4 %shard_map.198 = f32[32,1024]{1,0:T(8,128)} custom-call(s32[16,512]{1,0:T(8,128)} %add_bitcast_fusion.ids_ref, bf16[32,4096]{1,0:T(8,128)(2,1)} %feat_ref.1), custom_call_target="tpu_custom_call" | custom-call | flops 2684354560 | bytes 262144 | tf_op jit(solution)/shard_map/pallas_call | solution.py:62
  22.5 1.1 reshape.59
  23.6 0.1 slice.53
  23.7 0.2 convert_reduce_fusion.2
  23.9 0.6 fusion.7
  24.4 0.2 copy.27
  24.6 0.9 reshape.64
  25.5 7.3 %all-to-all-start = ((bf16[32,2,1024]{2,1,0:T(2,128)(2,1)}), bf16[32,2,1024]{2,1,0:T(2,128)(2,1)S(1)}, u32[]{:S(2)}, u32[]{:S(2)}) async-start(bf16[32,2,1024]{2,1,0:T(2,128)(2,1)} %reshape.64), calls=%async_computation | async-start | bytes 262144 | tf_op jit(solution)/shard_map/all_to_all | solution.py:128
  32.8 0.0 all-reduce.3.cloned.1.call-start
  32.8 0.6 broadcast_compare_fusion.9
  33.5 14.6 %all_gather.6 = bf16[128,1024]{1,0:T(8,128)(2,1)S(1)} all-gather(bf16[32,1024]{1,0:T(8,128)(2,1)S(1)} %copy-done.2), channel_id=1, replica_groups=mesh['feat'=4,'trainer'=8] {'feat'}, dimensions={0}, use_global_device_ids=true | all-gather | bytes 327680 | tf_op jit(solution)/shard_map/all_gather | solution.py:135
  48.1 15.4 %all_gather.7 = bf16[128,1024]{1,0:T(8,128)(2,1)} all-gather(bf16[32,1024]{1,0:T(8,128)(2,1)S(1)} %copy-done.3), channel_id=1, replica_groups=mesh['feat'=4,'trainer'=8] {'feat'}, dimensions={0}, use_global_device_ids=true | all-gather | bytes 327680 | tf_op jit(solution)/shard_map/all_gather | solution.py:136
  63.5 0.6 convert_element_type.81
  64.1 0.6 fusion.37
  64.7 0.2 reshape.65
  64.9 0.2 reshape.61
  65.2 0.5 copy.28
  65.7 0.0 copy-start.7
  65.7 0.4 reshape.62
  66.1 0.0 copy-start.26
  66.1 1.9 fusion.8
  68.0 0.5 convolution_convert_fusion.2
  68.5 0.0 copy-start.8
  68.5 0.0 copy-start.9
  68.5 0.0 copy-start.10
  68.6 0.0 copy-start.11
  68.6 0.0 copy-start.12
  68.6 0.0 copy-start.15
  68.7 1.3 fusion.39
  70.2 0.0 copy-start.27
  70.2 0.0 copy-start.28
  70.2 3.4 %divide_convert_fusion.1 = bf16[512,1024]{1,0:T(8,128)(2,1)S(1)} fusion(bf16[256,1024]{1,0:T(8,128)(2,1)S(1)} %fusion.8, f32[512]{0:T(512)S(1)} %copy-done.15, s32[512]{0:T(512)S(1)} %bitcast.77, s32[512]{0:T(512)S(1)} %bitcast.79, s32[512]{0:T(512)S(1)} %bitcast.63, s32[512]{0:T(512)S(1)} %bitcast.65, s32[512]{0:T(512)S(1)} %bitcast.67, ...), kind=kOutput, calls=%fused_computation.11 | convolution fusion | flops 274726912 | bytes 1600512 | tf_op jit(solution)/shard_map/dot_general | solution.py:154
  73.6 3.5 %convert_reduce_fusion = (f32[1024]{0:T(1024)S(1)}, bf16[512,1024]{1,0:T(8,128)(2,1)}, bf16[512,1024]{1,0:T(8,128)(2,1)}) fusion(bf16[512,1024]{1,0:T(8,128)(2,1)S(1)} %copy-done.27, f32[1024]{0:T(1024)S(1)} %copy-done.28, f32[512,1024]{1,0:T(8,128)S(1)} %fusion.39, bf16[512,1024]{1,0:T(8,128)(2,1)S(1)} %divide_convert_fusion.1, ...), kind=kOutput, calls=%fused_computation.6 | convolution fusion | flops 1082129408 | bytes 8396800 | tf_op jit(solution)/shard_map/dot_general | solution.py:158
  77.1 4.4 %fusion.6 = f32[256,1024]{1,0:T(8,128)} fusion(bf16[512,1024]{1,0:T(8,128)(2,1)} %get-tuple-element.10, bf16[1024,1024]{1,0:T(8,128)(2,1)S(1)} %copy-done, f32[512]{0:T(512)S(1)} %copy-done.15, s32[512]{0:T(512)S(1)} %bitcast.78, s32[512]{0:T(512)S(1)} %bitcast.80, s32[512]{0:T(512)S(1)} %bitcast.64, s32[512]{0:T(512)S(1)} %bitcast.66, ...), kind=kOutput, calls=%fused_computation.21 | convolution fusion | flops 1348468736 | bytes 4221952 | tf_op jit(solution)/shard_map/dot_general | solution.py:81
  81.5 5.9 %convolution_convert_fusion = bf16[2048,1024]{1,0:T(8,128)(2,1)} fusion(bf16[512,1024]{1,0:T(8,128)(2,1)} %get-tuple-element.10, bf16[512,1024]{1,0:T(8,128)(2,1)} %copy-done.29, bf16[512,1024]{1,0:T(8,128)(2,1)S(1)} %convolution_convert_fusion.2), kind=kOutput, calls=%fused_computation | convolution fusion | flops 2153775104 | bytes 7340032 | tf_op jit(solution)/shard_map/dot_general | solution.py:81
  87.4 4.0 %convert_reduce_fusion.1 = (f32[1024]{0:T(1024)S(1)}, bf16[256,1024]{1,0:T(8,128)(2,1)S(1)}) fusion(bf16[256,1024]{1,0:T(8,128)(2,1)} %copy-done.1, f32[256,1024]{1,0:T(8,128)} %fusion.6, bf16[512,1024]{1,0:T(8,128)(2,1)} %get-tuple-element.10, bf16[1024,1024]{1,0:T(8,128)(2,1)} %param.26, s32[512]{0:T(512)S(1)} %copy-done.7), kind=kOutput, calls=%fused_computation.24 | convolution fusion | flops 1344928768 | bytes 5249024 | tf_op jit(solution)/shard_map/dot_general | solution.py:81
  91.4 1.1 convolution_convert_fusion.3
  92.5 0.0 all-reduce.3.cloned.1.call-update
  92.5 39.9 %psum.22 = f32[2,1024]{1,0:T(2,128)S(1)} all-reduce(f32[2,1024]{1,0:T(2,128)S(1)} %pad_maximum_fusion), channel_id=1, replica_groups=mesh['feat'=4,'trainer'=8] {'feat','trainer'}, use_global_device_ids=true, to_apply=%region_4.5 | all-reduce | flops 2048 | bytes 16384 | tf_op jit(solution)/shard_map/psum | solution.py:183
  132.5 0.6 fusion.38
  133.1 105.1 %all-reduce.3.cloned.1.call-done = (bf16[2048,1024]{1,0:T(8,128)(2,1)}, bf16[2,4,32,1024]{3,2,1,0:T(8,128)(2,1)}) async-done(((bf16[2048,1024]{1,0:T(8,128)(2,1)}, bf16[2,4,32,1024]{3,2,1,0:T(8,128)(2,1)}), (bf16[2048,1024]{1,0:T(8,128)(2,1)}, bf16[2,4,32,1024]{3,2,1,0:T(8,128)(2,1)})) %all-reduce.3.cloned.1.call-update) | async-done | bytes 4718608 | tf_op jit(solution)/shard_map/psum | solution.py:166
  238.2 0.9 dynamic-slice_convert_fusion
  239.1 0.7 slice_bitcast_fusion
  239.8 6.7 %fusion.36 = (f32[1024,1024]{1,0:T(8,128)}, f32[1024,1024]{1,0:T(8,128)}) fusion(bf16[2048,1024]{1,0:T(8,128)(2,1)} %get-tuple-element.7), kind=kLoop, calls=%fused_computation.85 | loop fusion | bytes 16777216 | tf_op jit(solution)/shard_map/unstack | solution.py:185
  (55 shorter events, 0.2 us)
Async XLA Ops:
  7.2 66.4 %copy-start = (bf16[1024,1024]{1,0:T(8,128)(2,1)S(1)}, bf16[1024,1024]{1,0:T(8,128)(2,1)}, u32[]{:S(2)}) copy-start(bf16[1024,1024]{1,0:T(8,128)(2,1)} %param.27) | copy-start | bytes 6291460
  10.1 13.6 %copy-start.4 = (s32[512]{0:T(512)S(1)}, s32[512]{0:T(512)}, u32[]{:S(2)}) copy-start(s32[512]{0:T(512)} %param.19) | copy-start | bytes 6148
  22.4 10.4 %copy-start.6 = (s32[512]{0:T(512)S(1)}, s32[512]{0:T(512)}, u32[]{:S(2)}) copy-start(s32[512]{0:T(512)} %param.25) | copy-start | bytes 6148
  22.5 11.0 %copy-start.2 = (bf16[32,1024]{1,0:T(8,128)(2,1)S(1)}, bf16[32,1024]{1,0:T(8,128)(2,1)}, u32[]{:S(2)}) copy-start(bf16[32,1024]{1,0:T(8,128)(2,1)} %param.20) | copy-start | bytes 196612
  22.5 25.7 %copy-start.3 = (bf16[32,1024]{1,0:T(8,128)(2,1)S(1)}, bf16[32,1024]{1,0:T(8,128)(2,1)}, u32[]{:S(2)}) copy-start(bf16[32,1024]{1,0:T(8,128)(2,1)} %param.21) | copy-start | bytes 196612
  22.5 41.6 %copy-start.5 = (s32[512,10]{0,1:T(8,128)S(1)}, s32[512,10]{0,1:T(8,128)}, u32[]{:S(2)}) copy-start(s32[512,10]{0,1:T(8,128)} %param.23) | copy-start | bytes 61444
  25.5 39.2 %all-to-all-start = ((bf16[32,2,1024]{2,1,0:T(2,128)(2,1)}), bf16[32,2,1024]{2,1,0:T(2,128)(2,1)S(1)}, u32[]{:S(2)}, u32[]{:S(2)}) async-start(bf16[32,2,1024]{2,1,0:T(2,128)(2,1)} %reshape.64), calls=%async_computation | async-start | bytes 262144 | tf_op jit(solution)/shard_map/all_to_all | solution.py:128
  32.8 205.4 %all-reduce.3.cloned.1.call-start = ((), (), s32[]{:S(2)}) async-start(), calls=%async_computation.1 | async-start | bytes 9437184 | tf_op jit(solution)/shard_map/psum | solution.py:166
  65.7 2.3 copy-start.7
  66.1 2.4 copy-start.26
  68.0 1.9 copy-start.1
  68.5 1.5 copy-start.8
  68.5 1.5 copy-start.9
  68.5 1.5 copy-start.10
  68.6 1.5 copy-start.11
  68.6 1.5 copy-start.12
  68.6 1.4 copy-start.13
  68.6 1.4 copy-start.14
  68.6 1.4 copy-start.15
  68.6 1.4 copy-start.16
  68.6 1.4 copy-start.17
  68.6 1.4 copy-start.18
  68.6 1.4 copy-start.19
  68.6 1.4 copy-start.20
  68.7 1.4 copy-start.21
  68.7 1.4 copy-start.22
  68.7 1.4 copy-start.23
  68.7 1.4 copy-start.24
  68.7 1.4 copy-start.25
  70.2 3.4 %copy-start.27 = (bf16[512,1024]{1,0:T(8,128)(2,1)S(1)}, bf16[512,1024]{1,0:T(8,128)(2,1)}, u32[]{:S(2)}) copy-start(bf16[512,1024]{1,0:T(8,128)(2,1)} %param.29) | copy-start | bytes 3145732
  70.2 3.4 %copy-start.28 = (f32[1024]{0:T(1024)S(1)}, f32[1024]{0:T(1024)}, u32[]{:S(2)}) copy-start(f32[1024]{0:T(1024)} %param.28) | copy-start | bytes 12292
  73.6 3.5 %copy-start.29 = (bf16[512,1024]{1,0:T(8,128)(2,1)}, bf16[512,1024]{1,0:T(8,128)(2,1)S(1)}, u32[]{:S(2)}) copy-start(bf16[512,1024]{1,0:T(8,128)(2,1)S(1)} %divide_convert_fusion.1) | copy-start | bytes 3145732
Sparse Core Ops, SparseCore 0:
  92.6 145.5 all-reduce.2

commit v2 on v1

--- a/solution.py
+++ b/solution.py
@@ -8,6 +8,50 @@
 from jax.sharding import PartitionSpec as P
 
 CAP = 32
+
+
+def links():
+    def bits(axis):
+        return [(axis, bit) for bit in range(lax.axis_size(axis).bit_length() - 1)]
+
+    across, feat = bits("trainer"), bits("feat")
+    core, rest = across[:1], across[1:]
+    low, high = rest[: len(rest) // 2], rest[len(rest) // 2 :]
+    return core, low, high, feat
+
+
+def exchange(rows, link):
+    axis, bit = link
+    pairs = [(i, i ^ (1 << bit)) for i in range(lax.axis_size(axis))]
+    return lax.ppermute(rows, axis, pairs)
+
+
+def side(link):
+    axis, bit = link
+    return (lax.axis_index(axis) >> bit) & 1
+
+
+def scatter_step(rows, link):
+    half = rows.shape[0] // 2
+    mine = side(link)
+    kept = lax.dynamic_slice_in_dim(rows, mine * half, half, 0)
+    got = exchange(lax.dynamic_slice_in_dim(rows, (1 - mine) * half, half, 0), link)
+    return (kept.astype(jnp.float32) + got.astype(jnp.float32)).astype(jnp.bfloat16)
+
+
+def gather_step(rows, link):
+    got = exchange(rows, link)
+    first = side(link) == 0
+    return jnp.concatenate([jnp.where(first, rows, got), jnp.where(first, got, rows)], axis=0)
+
+
+def sum_parts(parts, orders):
+    steps = len(orders[0])
+    for step in range(steps):
+        parts = [scatter_step(part, order[step]) for part, order in zip(parts, orders)]
+    for step in reversed(range(steps)):
+        parts = [gather_step(part, order[step]) for part, order in zip(parts, orders)]
+    return parts
 
 
 CHUNK = 256
@@ -113,6 +157,10 @@
     block_width = features.shape[0]
     slot_total = owners_all * CAP
     slots = trainers * CAP
+    core, low, high, feat = links()
+    weights = jnp.concatenate([first_root, first_near], axis=0)
+    for link in feat:
+        weights = gather_step(weights, link)
     node_ids = jnp.arange(node_count, dtype=jnp.int32)
     earlier = (owner_map[:, None] == owner_map[None, :]) & (node_ids[:, None] < node_ids[None, :])
     slot_rank = jnp.sum(earlier.astype(jnp.int32), axis=0)
@@ -128,14 +176,10 @@
     arrived = lax.all_to_all(packed, ("feat", "trainer"), split_axis=1, concat_axis=1, tiled=True)
     arrived = (
         arrived.reshape(2, block_width, feat_size, trainers, CAP)
-        .transpose(0, 2, 1, 3, 4)
+        .transpose(2, 0, 1, 3, 4)
         .reshape(2 * feat_size * block_width, slots)
     )
-    root_all, near_all = (
-        lax.all_gather(first_root, "feat", axis=0, tiled=True),
-        lax.all_gather(first_near, "feat", axis=0, tiled=True),
-    )
-    pre_one = cross_rows(arrived, jnp.concatenate([root_all, near_all], axis=0)) + first_bias
+    pre_one = cross_rows(arrived, weights) + first_bias
     hidden_table = jax.nn.softplus(pre_one).astype(jnp.bfloat16)
     slot_ids = jnp.arange(slots, dtype=jnp.int32)
     root_pick = (second_center[:, None] == slot_ids[None, :]).astype(jnp.bfloat16)
@@ -163,7 +207,14 @@
         jnp.bfloat16
     )
     both = jnp.concatenate([root_rows, near_two], axis=1)
-    grad_two = lax.psum(cross_rows(both, slope_two).astype(jnp.bfloat16), ("feat", "trainer"))
+    grad_two = cross_rows(both, slope_two).astype(jnp.bfloat16)
+    units = grad_two.shape[0] // owners_all
+    ends = [(units * part // 3) * owners_all for part in range(4)]
+    grad_two = sum_parts(
+        [grad_two[ends[part] : ends[part + 1]] for part in range(3)],
+        [core + low + high + feat, core + high + feat + low, core + feat + low + high],
+    )
+    grad_two = jnp.concatenate(grad_two, axis=0)
     back_root = cross_cols(slope_two, second_root).astype(jnp.bfloat16)
     back_near = (cross_cols(slope_two, second_near) / divisor).astype(jnp.bfloat16)
     table_grad = cross_rows(root_pick, back_root) + cross_rows(multiples, back_near)
@@ -171,16 +222,20 @@
         jnp.bfloat16
     )
     grad_one = jnp.dot(arrived, pre_grad, preferred_element_type=jnp.float32)
-    grad_one = grad_one.astype(jnp.bfloat16).reshape(2, feat_size, block_width, -1)
-    grad_one = lax.psum(grad_one, ("feat", "trainer"))
-    grad_one = lax.dynamic_index_in_dim(grad_one, lax.axis_index("feat"), 1, keepdims=False)
+    grad_one = grad_one.astype(jnp.bfloat16)
+    for link in reversed(feat):
+        grad_one = scatter_step(grad_one, link)
+    (grad_one,) = sum_parts([grad_one], [core + low + high])
+    grad_one = grad_one.reshape(2, block_width, -1)
     biases = jnp.stack(
         [
             jnp.sum(slope_two.astype(jnp.float32), axis=0),
             jnp.sum(pre_grad.astype(jnp.float32), axis=0),
         ]
     )
-    biasgrad_two, biasgrad_one = lax.psum(biases, ("feat", "trainer"))
+    for link in core + low + high + feat:
+        biases = biases + exchange(biases, link)
+    biasgrad_two, biasgrad_one = biases
     grad_two = grad_two.astype(jnp.float32).reshape(2, -1, grad_two.shape[1])
     rootgrad_two, neargrad_two = grad_two
     rootgrad_one, neargrad_one = grad_one.astype(jnp.float32)

time: 254 us -> 185 us (0.73)
  blocking collectives: 70 us -> 0 us
  starting transfers between devices: 7.34 us -> 46 us
  waiting for transfers between devices: 105 us -> 75.3 us
  between operations: 14.6 us -> 1.91 us
  other arithmetic: 5.23 us -> 10.7 us
    psum x1 -> x0, waiting for transfers between devices: 105 us -> none  [local(): lax.psum(cross_rows(both, slope_two).astype(jnp.bfloat16), ('feat', 'trai...]
    ppermute x0 -> x45, waiting for transfers between devices: none -> 67.9 us  [exchange(): return lax.ppermute(rows, axis, pairs)]
    ppermute x0 -> x45, starting transfers between devices: none -> 41.2 us  [exchange(): return lax.ppermute(rows, axis, pairs)]
    psum x1 -> x0, blocking collectives: 39.9 us -> none  [local(): biasgrad_two, biasgrad_one = lax.psum(biases, ('feat', 'trainer'))]
    all_gather x2 -> x0, blocking collectives: 30 us -> none  [the longest x1 15.4 us: local(): lax.all_gather(first_near, 'feat', axis=0, tiled=True)]
    all_to_all x1, waiting for transfers between devices: 0.01 us -> 7.37 us  [local(): lax.all_to_all(packed, ('feat', 'trainer'), split_axis=1, concat_axis=1,...]
  transfers between devices with their start and end apart: 2 -> 46, of which waited for: 1 -> 31; matrix products, arithmetic and copies ran while one was open for 1% -> 12% of each run, Pallas kernels for 0% -> 7%
where the time goes in v2:
time: 185 us; the launch traced here: 184 us
  waiting for transfers between devices  75.3 us (41%)
  starting transfers between devices  46 us (25%)
  matrix products  25.3 us (14%)
  local copies, waits for them, and re-layouts  12.9 us (7%)
  Pallas kernels  12.4 us (7%)
  other arithmetic  10.7 us (6%)
  between operations  1.91 us (1%)
    ppermute x45, waiting for transfers between devices, exchange(): return lax.ppermute(rows, axis, pairs)  67.9 us
    ppermute x45, starting transfers between devices, exchange(): return lax.ppermute(rows, axis, pairs)  41.2 us
    dot_general x4, matrix products, cross_rows(): lax.dot_general(left, right, (((0,), (0,)), ((), ())), preferred_element_...  14.7 us
    pallas_call x1, Pallas kernels, select(): pl.pallas_call(functools.partial(select_kernel, fanout), grid=(steps,), i...  12.4 us
    all_to_all x1, waiting for transfers between devices, local(): lax.all_to_all(packed, ('feat', 'trainer'), split_axis=1, concat_axis=1,...  7.37 us
    all_to_all x1, starting transfers between devices, local(): lax.all_to_all(packed, ('feat', 'trainer'), split_axis=1, concat_axis=1,...  4.84 us
    another operation x1, local copies, waits for them, and re-layouts, local(): rootgrad_two, neargrad_two = grad_two  4.43 us
  transfers between devices with their start and end apart: 46, of which 31 were waited for; matrix products, arithmetic and copies ran while one was open for 12% of the time, Pallas kernels for 7%

profile of v2, /device:TPU:0, one launch (start us, length us, event | category | flops | bytes accessed | tf_op | source)
XLA Modules:
  0.0 184.4 jit_solution(5903252785776781383)
XLA Ops:
  2.5 3.0 %collective-permute-start = (bf16[64,1024]{1,0:T(8,128)(2,1)S(1)}, bf16[64,1024]{1,0:T(8,128)(2,1)S(1)}, u32[]{:S(2)}, u32[]{:S(2)}) collective-permute-start(bf16[64,1024]{1,0:T(8,128)(2,1)S(1)} %constant_dynamic-update-slice_fusion), channel_id=1, source_target_pairs={{0,8},{8,0},{16,24},{24,16},{1,9},{9,1},{17,25},{25,17},{2,10},{10... | collective-permute-start | bytes 393224 | tf_op jit(solution)/shard_map/ppermute | solution.py:26
  7.0 1.3 add_bitcast_fusion.ids_ref
  8.3 12.4 %shard_map.198 = f32[32,1024]{1,0:T(8,128)} custom-call(s32[16,512]{1,0:T(8,128)} %add_bitcast_fusion.ids_ref, bf16[32,4096]{1,0:T(8,128)(2,1)} %feat_ref.1), custom_call_target="tpu_custom_call" | custom-call | flops 2684354560 | bytes 262144 | tf_op jit(solution)/shard_map/pallas_call | solution.py:106
  23.6 4.8 %all-to-all-start = ((bf16[32,2,1024]{2,1,0:T(2,128)(2,1)}), bf16[32,2,1024]{2,1,0:T(2,128)(2,1)S(1)}, u32[]{:S(2)}, u32[]{:S(2)}) async-start(bf16[32,2,1024]{2,1,0:T(2,128)(2,1)} %reshape.61), calls=%async_computation | async-start | bytes 262144 | tf_op jit(solution)/shard_map/all_to_all | solution.py:176
  29.2 2.7 %collective-permute-start.1 = (bf16[128,1024]{1,0:T(8,128)(2,1)}, bf16[128,1024]{1,0:T(8,128)(2,1)}, u32[]{:S(2)}, u32[]{:S(2)}) collective-permute-start(bf16[128,1024]{1,0:T(8,128)(2,1)} %pad_maximum_fusion.6), channel_id=1, source_target_pairs={{0,16},{8,24},{16,0},{24,8},{1,17},{9,25},{17,1},{25,9},{2,18},{10... | collective-permute-start | bytes 786440 | tf_op jit(solution)/shard_map/ppermute | solution.py:26
  33.7 7.4 %all-to-all-done = bf16[32,2,1024]{2,1,0:T(2,128)(2,1)S(1)} async-done(((bf16[32,2,1024]{2,1,0:T(2,128)(2,1)}), bf16[32,2,1024]{2,1,0:T(2,128)(2,1)S(1)}, u32[]{:S(2)}, u32[]{:S(2)}) %all-to-all-start) | async-done | bytes 131104 | tf_op jit(solution)/shard_map/all_to_all | solution.py:176
  42.5 3.9 %collective-permute-done.1 = bf16[128,1024]{1,0:T(8,128)(2,1)} collective-permute-done((bf16[128,1024]{1,0:T(8,128)(2,1)}, bf16[128,1024]{1,0:T(8,128)(2,1)}, u32[]{:S(2)}, u32[]{:S(2)}) %collective-permute-start.1) | collective-permute-done | bytes 262176 | tf_op jit(solution)/shard_map/ppermute | solution.py:26
  47.5 1.6 fusion.8
  49.8 1.2 fusion.42
  51.3 3.6 %divide_convert_fusion.1 = bf16[512,1024]{1,0:T(8,128)(2,1)S(1)} fusion(bf16[256,1024]{1,0:T(8,128)(2,1)S(1)} %fusion.8, f32[512]{0:T(512)S(1)} %copy-done.12, s32[512]{0:T(512)S(1)} %bitcast.75, s32[512]{0:T(512)S(1)} %bitcast.77, s32[512]{0:T(512)S(1)} %bitcast.61, s32[512]{0:T(512)S(1)} %bitcast.63, s32[512]{0:T(512)S(1)} %bitcast.65, ...), kind=kOutput, calls=%fused_computation.11 | convolution fusion | flops 274726912 | bytes 1600512 | tf_op jit(solution)/shard_map/dot_general | solution.py:198
  54.9 3.5 %convert_reduce_fusion = (f32[1024]{0:T(1024)S(1)}, bf16[512,1024]{1,0:T(8,128)(2,1)}, bf16[512,1024]{1,0:T(8,128)(2,1)}) fusion(bf16[512,1024]{1,0:T(8,128)(2,1)S(1)} %copy-done.24, f32[1024]{0:T(1024)S(1)} %copy-done.25, f32[512,1024]{1,0:T(8,128)S(1)} %fusion.42, bf16[512,1024]{1,0:T(8,128)(2,1)S(1)} %divide_convert_fusion.1, ...), kind=kOutput, calls=%fused_computation.6 | convolution fusion | flops 1082129408 | bytes 8396800 | tf_op jit(solution)/shard_map/dot_general | solution.py:202
  58.3 4.4 %fusion.6 = f32[256,1024]{1,0:T(8,128)} fusion(bf16[512,1024]{1,0:T(8,128)(2,1)} %get-tuple-element.8, bf16[1024,1024]{1,0:T(8,128)(2,1)S(1)} %copy-done, f32[512]{0:T(512)S(1)} %copy-done.12, s32[512]{0:T(512)S(1)} %bitcast.76, s32[512]{0:T(512)S(1)} %bitcast.78, s32[512]{0:T(512)S(1)} %bitcast.62, s32[512]{0:T(512)S(1)} %bitcast.64, s32[512]{0:T(512)S(1)} %bitcast.66, ...), kind=kOutput, calls=%fused_computation.24 | convolution fusion | flops 1348468736 | bytes 4221952 | tf_op jit(solution)/shard_map/dot_general | solution.py:125
  62.7 4.8 %convert_reduce_fusion.1 = (f32[1024]{0:T(1024)S(1)}, bf16[256,1024]{1,0:T(8,128)(2,1)}) fusion(bf16[256,1024]{1,0:T(8,128)(2,1)} %copy-done.1, f32[256,1024]{1,0:T(8,128)} %fusion.6, bf16[512,1024]{1,0:T(8,128)(2,1)} %get-tuple-element.8, bf16[1024,1024]{1,0:T(8,128)(2,1)} %param.26, s32[512]{0:T(512)S(1)} %copy-done.5), kind=kOutput, calls=%fused_computation.27 | convolution fusion | flops 1344928768 | bytes 5249024 | tf_op jit(solution)/shard_map/dot_general | solution.py:125
  67.6 1.3 convolution_convert_fusion.3
  69.0 3.9 %convolution_convert_fusion = bf16[2048,1024]{1,0:T(8,128)(2,1)S(1)} fusion(bf16[512,1024]{1,0:T(8,128)(2,1)} %get-tuple-element.8, bf16[512,1024]{1,0:T(8,128)(2,1)} %copy-done.26, bf16[512,1024]{1,0:T(8,128)(2,1)S(1)} %convolution_convert_fusion.2), kind=kOutput, calls=%fused_computation | convolution fusion | flops 2153775104 | bytes 7340032 | tf_op jit(solution)/shard_map/dot_general | solution.py:125
  73.0 10.3 %collective-permute-done.37 = bf16[128,1024]{1,0:T(8,128)(2,1)S(1)} collective-permute-done((bf16[128,1024]{1,0:T(8,128)(2,1)S(1)}, bf16[128,1024]{1,0:T(8,128)(2,1)S(1)}, u32[]{:S(2)}, u32[]{:S(2)}) %collective-permute-start.37) | collective-permute-done | bytes 262176 | tf_op jit(solution)/shard_map/ppermute | solution.py:26
  83.7 5.2 %collective-permute-done.38 = bf16[64,1024]{1,0:T(8,128)(2,1)S(1)} collective-permute-done((bf16[64,1024]{1,0:T(8,128)(2,1)S(1)}, bf16[64,1024]{1,0:T(8,128)(2,1)S(1)}, u32[]{:S(2)}, u32[]{:S(2)}) %collective-permute-start.38) | collective-permute-done | bytes 131104 | tf_op jit(solution)/shard_map/ppermute | solution.py:26
  89.0 1.5 collective-permute-start.33
  90.6 1.2 collective-permute-start.40
  92.8 1.5 collective-permute-start.34
  94.6 1.6 collective-permute-start.41
  96.9 1.6 collective-permute-done.41
  98.4 1.6 collective-permute-start.42
  102.2 1.3 collective-permute-start.43
  103.6 1.7 collective-permute-done.36
  108.7 1.3 collective-permute-start.3
  110.2 1.5 collective-permute-start.13
  113.1 5.7 %collective-permute-done.3 = bf16[168,1024]{1,0:T(8,128)(2,1)S(1)} collective-permute-done((bf16[168,1024]{1,0:T(8,128)(2,1)S(1)}, bf16[168,1024]{1,0:T(8,128)(2,1)S(1)}, u32[]{:S(2)}, u32[]{:S(2)}) %collective-permute-start.3) | collective-permute-done | bytes 344096 | tf_op jit(solution)/shard_map/ppermute | solution.py:26
  119.0 1.6 collective-permute-start.4
  122.2 1.8 %collective-permute-start.24 = (bf16[88,1024]{1,0:T(8,128)(2,1)S(1)}, bf16[88,1024]{1,0:T(8,128)(2,1)S(1)}, u32[]{:S(2)}, u32[]{:S(2)}) collective-permute-start(bf16[88,1024]{1,0:T(8,128)(2,1)S(1)} %constant_dynamic-slice_fusion.7), channel_id=1, source_target_pairs={{0,16},{8,24},{16,0},{24,8},{1,17},{9,25},{17,1},{25,9},{2,18},{10... | collective-permute-start | bytes 540680 | tf_op jit(solution)/shard_map/ppermute | solution.py:26
  125.0 1.4 collective-permute-start.5
  126.4 3.7 %collective-permute-done.14 = bf16[84,1024]{1,0:T(8,128)(2,1)S(1)} collective-permute-done((bf16[84,1024]{1,0:T(8,128)(2,1)S(1)}, bf16[84,1024]{1,0:T(8,128)(2,1)S(1)}, u32[]{:S(2)}, u32[]{:S(2)}) %collective-permute-start.14) | collective-permute-done | bytes 172064 | tf_op jit(solution)/shard_map/ppermute | solution.py:26
  130.3 6.1 %collective-permute-done.24 = bf16[88,1024]{1,0:T(8,128)(2,1)S(1)} collective-permute-done((bf16[88,1024]{1,0:T(8,128)(2,1)S(1)}, bf16[88,1024]{1,0:T(8,128)(2,1)S(1)}, u32[]{:S(2)}, u32[]{:S(2)}) %collective-permute-start.24) | collective-permute-done | bytes 180256 | tf_op jit(solution)/shard_map/ppermute | solution.py:26
  137.7 1.2 collective-permute-start.16
  138.9 3.2 %collective-permute-done.6 = bf16[21,1024]{1,0:T(8,128)(2,1)S(1)} collective-permute-done((bf16[21,1024]{1,0:T(8,128)(2,1)S(1)}, bf16[21,1024]{1,0:T(8,128)(2,1)S(1)}, u32[]{:S(2)}, u32[]{:S(2)}) %collective-permute-start.6) | collective-permute-done | bytes 43040 | tf_op jit(solution)/shard_map/ppermute | solution.py:26
  142.3 1.8 collective-permute-start.17
  144.3 4.6 %collective-permute-done.7 = bf16[21,1024]{1,0:T(8,128)(2,1)S(1)} collective-permute-done((bf16[21,1024]{1,0:T(8,128)(2,1)S(1)}, bf16[21,1024]{1,0:T(8,128)(2,1)S(1)}, u32[]{:S(2)}, u32[]{:S(2)}) %collective-permute-start.7) | collective-permute-done | bytes 43040 | tf_op jit(solution)/shard_map/ppermute | solution.py:26
  149.2 2.8 %collective-permute-start.18 = (bf16[42,1024]{1,0:T(8,128)(2,1)S(1)}, bf16[42,1024]{1,0:T(8,128)(2,1)S(1)}, u32[]{:S(2)}, u32[]{:S(2)}) collective-permute-start(bf16[42,1024]{1,0:T(8,128)(2,1)S(1)} %pad_maximum_fusion.11), channel_id=1, source_target_pairs={{0,16},{8,24},{16,0},{24,8},{1,17},{9,25},{17,1},{25,9},{2,18},{10... | collective-permute-start | bytes 258056 | tf_op jit(solution)/shard_map/ppermute | solution.py:26
  153.2 1.6 collective-permute-start.28
  154.9 1.9 %collective-permute-done.8 = bf16[42,1024]{1,0:T(8,128)(2,1)S(1)} collective-permute-done((bf16[42,1024]{1,0:T(8,128)(2,1)S(1)}, bf16[42,1024]{1,0:T(8,128)(2,1)S(1)}, u32[]{:S(2)}, u32[]{:S(2)}) %collective-permute-start.8) | collective-permute-done | bytes 86048 | tf_op jit(solution)/shard_map/ppermute | solution.py:26
  157.0 1.8 collective-permute-done.18
  159.1 2.8 %collective-permute-start.29 = (bf16[88,1024]{1,0:T(8,128)(2,1)S(1)}, bf16[88,1024]{1,0:T(8,128)(2,1)S(1)}, u32[]{:S(2)}, u32[]{:S(2)}) collective-permute-start(bf16[88,1024]{1,0:T(8,128)(2,1)S(1)} %pad_maximum_fusion.9), channel_id=1, source_target_pairs={{0,16},{8,24},{16,0},{24,8},{1,17},{9,25},{17,1},{25,9},{2,18},{10... | collective-permute-start | bytes 540680 | tf_op jit(solution)/shard_map/ppermute | solution.py:26
  161.9 2.4 %collective-permute-done.9 = bf16[84,1024]{1,0:T(8,128)(2,1)S(1)} collective-permute-done((bf16[84,1024]{1,0:T(8,128)(2,1)S(1)}, bf16[84,1024]{1,0:T(8,128)(2,1)S(1)}, u32[]{:S(2)}, u32[]{:S(2)}) %collective-permute-start.9) | collective-permute-done | bytes 172064 | tf_op jit(solution)/shard_map/ppermute | solution.py:26
  164.5 1.6 collective-permute-start.10
  166.1 2.1 %collective-permute-done.19 = bf16[84,1024]{1,0:T(8,128)(2,1)S(1)} collective-permute-done((bf16[84,1024]{1,0:T(8,128)(2,1)S(1)}, bf16[84,1024]{1,0:T(8,128)(2,1)S(1)}, u32[]{:S(2)}, u32[]{:S(2)}) %collective-permute-start.19) | collective-permute-done | bytes 172064 | tf_op jit(solution)/shard_map/ppermute | solution.py:26
  169.5 1.2 collective-permute-start.30
  172.1 3.6 %collective-permute-done.20 = bf16[168,1024]{1,0:T(8,128)(2,1)S(1)} collective-permute-done((bf16[168,1024]{1,0:T(8,128)(2,1)S(1)}, bf16[168,1024]{1,0:T(8,128)(2,1)S(1)}, u32[]{:S(2)}, u32[]{:S(2)}) %collective-permute-start.20) | collective-permute-done | bytes 344096 | tf_op jit(solution)/shard_map/ppermute | solution.py:26
  180.0 4.4 %fusion.37 = (f32[1024,1024]{1,0:T(8,128)}, f32[1024,1024]{1,0:T(8,128)}) fusion(bf16[2048,1024]{1,0:T(8,128)(2,1)S(1)} %select_dynamic-update-slice_fusion), kind=kLoop, calls=%fused_computation.181 | loop fusion | bytes 16777216 | tf_op jit(solution)/shard_map/unstack | solution.py:240
  (220 shorter events, 35.1 us)
Async XLA Ops:
  0.6 54.2 %copy-start = (bf16[1024,1024]{1,0:T(8,128)(2,1)S(1)}, bf16[1024,1024]{1,0:T(8,128)(2,1)}, u32[]{:S(2)}) copy-start(bf16[1024,1024]{1,0:T(8,128)(2,1)} %param.27) | copy-start | bytes 6291460
  2.5 26.0 %collective-permute-start = (bf16[64,1024]{1,0:T(8,128)(2,1)S(1)}, bf16[64,1024]{1,0:T(8,128)(2,1)S(1)}, u32[]{:S(2)}, u32[]{:S(2)}) collective-permute-start(bf16[64,1024]{1,0:T(8,128)(2,1)S(1)} %constant_dynamic-update-slice_fusion), channel_id=1, source_target_pairs={{0,8},{8,0},{16,24},{24,16},{1,9},{9,1},{17,25},{25,17},{2,10},{10... | collective-permute-start | bytes 393224 | tf_op jit(solution)/shard_map/ppermute | solution.py:26
  8.3 13.5 %copy-start.2 = (s32[512]{0:T(512)S(1)}, s32[512]{0:T(512)}, u32[]{:S(2)}) copy-start(s32[512]{0:T(512)} %param.19) | copy-start | bytes 6148
  23.6 17.5 %all-to-all-start = ((bf16[32,2,1024]{2,1,0:T(2,128)(2,1)}), bf16[32,2,1024]{2,1,0:T(2,128)(2,1)S(1)}, u32[]{:S(2)}, u32[]{:S(2)}) async-start(bf16[32,2,1024]{2,1,0:T(2,128)(2,1)} %reshape.61), calls=%async_computation | async-start | bytes 262144 | tf_op jit(solution)/shard_map/all_to_all | solution.py:176
  29.2 17.1 %collective-permute-start.1 = (bf16[128,1024]{1,0:T(8,128)(2,1)}, bf16[128,1024]{1,0:T(8,128)(2,1)}, u32[]{:S(2)}, u32[]{:S(2)}) collective-permute-start(bf16[128,1024]{1,0:T(8,128)(2,1)} %pad_maximum_fusion.6), channel_id=1, source_target_pairs={{0,16},{8,24},{16,0},{24,8},{1,17},{9,25},{17,1},{25,9},{2,18},{10... | collective-permute-start | bytes 786440 | tf_op jit(solution)/shard_map/ppermute | solution.py:26
  67.5 21.5 %collective-permute-start.32 = (f32[2,1024]{1,0:T(2,128)S(1)}, f32[2,1024]{1,0:T(2,128)S(1)}, u32[]{:S(2)}, u32[]{:S(2)}) collective-permute-start(f32[2,1024]{1,0:T(2,128)S(1)} %pad_maximum_fusion.15), channel_id=1, source_target_pairs={{0,1},{1,0},{2,3},{3,2},{4,5},{5,4},{6,7},{7,6},{8,9},{9,8},{10,11... | collective-permute-start | bytes 24584 | tf_op jit(solution)/shard_map/ppermute | solution.py:26
  68.9 14.3 %collective-permute-start.37 = (bf16[128,1024]{1,0:T(8,128)(2,1)S(1)}, bf16[128,1024]{1,0:T(8,128)(2,1)S(1)}, u32[]{:S(2)}, u32[]{:S(2)}) collective-permute-start(bf16[128,1024]{1,0:T(8,128)(2,1)S(1)} %constant_dynamic-slice_fusion.4), channel_id=1, source_target_pairs={{0,16},{8,24},{16,0},{24,8},{1,17},{9,25},{17,1},{25,9},{2,18},{10... | collective-permute-start | bytes 786440 | tf_op jit(solution)/shard_map/ppermute | solution.py:26
  83.3 5.5 %collective-permute-start.38 = (bf16[64,1024]{1,0:T(8,128)(2,1)S(1)}, bf16[64,1024]{1,0:T(8,128)(2,1)S(1)}, u32[]{:S(2)}, u32[]{:S(2)}) collective-permute-start(bf16[64,1024]{1,0:T(8,128)(2,1)S(1)} %constant_dynamic-slice_fusion.3), channel_id=1, source_target_pairs={{0,8},{8,0},{16,24},{24,16},{1,9},{9,1},{17,25},{25,17},{2,10},{10... | collective-permute-start | bytes 393224 | tf_op jit(solution)/shard_map/ppermute | solution.py:26
  88.9 1.6 collective-permute-start.39
  89.0 3.7 %collective-permute-start.33 = (f32[2,1024]{1,0:T(2,128)S(1)}, f32[2,1024]{1,0:T(2,128)S(1)}, u32[]{:S(2)}, u32[]{:S(2)}) collective-permute-start(f32[2,1024]{1,0:T(2,128)S(1)} %fusion.36), channel_id=1, source_target_pairs={{0,2},{1,3},{2,0},{3,1},{4,6},{5,7},{6,4},{7,5},{8,10},{9,11},{10,... | collective-permute-start | bytes 24584 | tf_op jit(solution)/shard_map/ppermute | solution.py:26
  90.6 4.0 %collective-permute-start.40 = (bf16[16,1024]{1,0:T(8,128)(2,1)S(1)}, bf16[16,1024]{1,0:T(8,128)(2,1)S(1)}, u32[]{:S(2)}, u32[]{:S(2)}) collective-permute-start(bf16[16,1024]{1,0:T(8,128)(2,1)S(1)} %constant_dynamic-slice_fusion.1), channel_id=1, source_target_pairs={{0,2},{1,3},{2,0},{3,1},{4,6},{5,7},{6,4},{7,5},{8,10},{9,11},{10,... | collective-permute-start | bytes 98312 | tf_op jit(solution)/shard_map/ppermute | solution.py:26
  92.8 3.8 %collective-permute-start.34 = (f32[2,1024]{1,0:T(2,128)S(1)}, f32[2,1024]{1,0:T(2,128)S(1)}, u32[]{:S(2)}, u32[]{:S(2)}) collective-permute-start(f32[2,1024]{1,0:T(2,128)S(1)} %fusion.57), channel_id=1, source_target_pairs={{0,4},{1,5},{2,6},{3,7},{4,0},{5,1},{6,2},{7,3},{8,12},{9,13},{10,... | collective-permute-start | bytes 24584 | tf_op jit(solution)/shard_map/ppermute | solution.py:26
  94.6 3.8 %collective-permute-start.41 = (bf16[8,1024]{1,0:T(8,128)(2,1)S(1)}, bf16[8,1024]{1,0:T(8,128)(2,1)S(1)}, u32[]{:S(2)}, u32[]{:S(2)}) collective-permute-start(bf16[8,1024]{1,0:T(8,128)(2,1)S(1)} %constant_dynamic-slice_fusion), channel_id=1, source_target_pairs={{0,4},{1,5},{2,6},{3,7},{4,0},{5,1},{6,2},{7,3},{8,12},{9,13},{10,... | collective-permute-start | bytes 49160 | tf_op jit(solution)/shard_map/ppermute | solution.py:26
  96.6 4.2 %collective-permute-start.35 = (f32[2,1024]{1,0:T(2,128)S(1)}, f32[2,1024]{1,0:T(2,128)S(1)}, u32[]{:S(2)}, u32[]{:S(2)}) collective-permute-start(f32[2,1024]{1,0:T(2,128)S(1)} %add.317), channel_id=1, source_target_pairs={{0,8},{8,0},{16,24},{24,16},{1,9},{9,1},{17,25},{25,17},{2,10},{10... | collective-permute-start | bytes 24584 | tf_op jit(solution)/shard_map/ppermute | solution.py:26
  98.4 3.8 %collective-permute-start.42 = (bf16[8,1024]{1,0:T(8,128)(2,1)S(1)}, bf16[8,1024]{1,0:T(8,128)(2,1)S(1)}, u32[]{:S(2)}, u32[]{:S(2)}) collective-permute-start(bf16[8,1024]{1,0:T(8,128)(2,1)S(1)} %add_convert_fusion.20), channel_id=1, source_target_pairs={{0,4},{1,5},{2,6},{3,7},{4,0},{5,1},{6,2},{7,3},{8,12},{9,13},{10,... | collective-permute-start | bytes 49160 | tf_op jit(solution)/shard_map/ppermute | solution.py:26
  100.2 8.2 %collective-permute-start.2 = (bf16[336,1024]{1,0:T(8,128)(2,1)S(1)}, bf16[336,1024]{1,0:T(8,128)(2,1)S(1)}, u32[]{:S(2)}, u32[]{:S(2)}) collective-permute-start(bf16[336,1024]{1,0:T(8,128)(2,1)S(1)} %constant_dynamic-slice_fusion.19), channel_id=1, source_target_pairs={{0,1},{1,0},{2,3},{3,2},{4,5},{5,4},{6,7},{7,6},{8,9},{9,8},{10,11... | collective-permute-start | bytes 2064392 | tf_op jit(solution)/shard_map/ppermute | solution.py:26
  100.2 9.7 %collective-permute-start.12 = (bf16[336,1024]{1,0:T(8,128)(2,1)S(1)}, bf16[336,1024]{1,0:T(8,128)(2,1)S(1)}, u32[]{:S(2)}, u32[]{:S(2)}) collective-permute-start(bf16[336,1024]{1,0:T(8,128)(2,1)S(1)} %constant_dynamic-slice_fusion.14), channel_id=1, source_target_pairs={{0,1},{1,0},{2,3},{3,2},{4,5},{5,4},{6,7},{7,6},{8,9},{9,8},{10,11... | collective-permute-start | bytes 2064392 | tf_op jit(solution)/shard_map/ppermute | solution.py:26
  100.7 4.6 %collective-permute-start.36 = (f32[2,1024]{1,0:T(2,128)S(1)}, f32[2,1024]{1,0:T(2,128)S(1)}, u32[]{:S(2)}, u32[]{:S(2)}) collective-permute-start(f32[2,1024]{1,0:T(2,128)S(1)} %add.318), channel_id=1, source_target_pairs={{0,16},{8,24},{16,0},{24,8},{1,17},{9,25},{17,1},{25,9},{2,18},{10... | collective-permute-start | bytes 24584 | tf_op jit(solution)/shard_map/ppermute | solution.py:26
  102.2 4.0 %collective-permute-start.43 = (bf16[16,1024]{1,0:T(8,128)(2,1)S(1)}, bf16[16,1024]{1,0:T(8,128)(2,1)S(1)}, u32[]{:S(2)}, u32[]{:S(2)}) collective-permute-start(bf16[16,1024]{1,0:T(8,128)(2,1)S(1)} %pad_maximum_fusion.14), channel_id=1, source_target_pairs={{0,2},{1,3},{2,0},{3,1},{4,6},{5,7},{6,4},{7,5},{8,10},{9,11},{10,... | collective-permute-start | bytes 98312 | tf_op jit(solution)/shard_map/ppermute | solution.py:26
  103.6 8.2 %collective-permute-start.22 = (bf16[352,1024]{1,0:T(8,128)(2,1)S(1)}, bf16[352,1024]{1,0:T(8,128)(2,1)S(1)}, u32[]{:S(2)}, u32[]{:S(2)}) collective-permute-start(bf16[352,1024]{1,0:T(8,128)(2,1)S(1)} %constant_dynamic-slice_fusion.9), channel_id=1, source_target_pairs={{0,1},{1,0},{2,3},{3,2},{4,5},{5,4},{6,7},{7,6},{8,9},{9,8},{10,11... | collective-permute-start | bytes 2162696 | tf_op jit(solution)/shard_map/ppermute | solution.py:26
  106.3 1.3 collective-permute-start.44
  108.7 10.2 %collective-permute-start.3 = (bf16[168,1024]{1,0:T(8,128)(2,1)S(1)}, bf16[168,1024]{1,0:T(8,128)(2,1)S(1)}, u32[]{:S(2)}, u32[]{:S(2)}) collective-permute-start(bf16[168,1024]{1,0:T(8,128)(2,1)S(1)} %constant_dynamic-slice_fusion.18), channel_id=1, source_target_pairs={{0,2},{1,3},{2,0},{3,1},{4,6},{5,7},{6,4},{7,5},{8,10},{9,11},{10,... | collective-permute-start | bytes 1032200 | tf_op jit(solution)/shard_map/ppermute | solution.py:26
  110.2 10.4 %collective-permute-start.13 = (bf16[168,1024]{1,0:T(8,128)(2,1)S(1)}, bf16[168,1024]{1,0:T(8,128)(2,1)S(1)}, u32[]{:S(2)}, u32[]{:S(2)}) collective-permute-start(bf16[168,1024]{1,0:T(8,128)(2,1)S(1)} %constant_dynamic-slice_fusion.13), channel_id=1, source_target_pairs={{0,4},{1,5},{2,6},{3,7},{4,0},{5,1},{6,2},{7,3},{8,12},{9,13},{10,... | collective-permute-start | bytes 1032200 | tf_op jit(solution)/shard_map/ppermute | solution.py:26
  112.0 10.0 %collective-permute-start.23 = (bf16[176,1024]{1,0:T(8,128)(2,1)S(1)}, bf16[176,1024]{1,0:T(8,128)(2,1)S(1)}, u32[]{:S(2)}, u32[]{:S(2)}) collective-permute-start(bf16[176,1024]{1,0:T(8,128)(2,1)S(1)} %constant_dynamic-slice_fusion.8), channel_id=1, source_target_pairs={{0,8},{8,0},{16,24},{24,16},{1,9},{9,1},{17,25},{25,17},{2,10},{10... | collective-permute-start | bytes 1081352 | tf_op jit(solution)/shard_map/ppermute | solution.py:26
  119.0 5.8 %collective-permute-start.4 = (bf16[84,1024]{1,0:T(8,128)(2,1)S(1)}, bf16[84,1024]{1,0:T(8,128)(2,1)S(1)}, u32[]{:S(2)}, u32[]{:S(2)}) collective-permute-start(bf16[84,1024]{1,0:T(8,128)(2,1)S(1)} %constant_dynamic-slice_fusion.17), channel_id=1, source_target_pairs={{0,4},{1,5},{2,6},{3,7},{4,0},{5,1},{6,2},{7,3},{8,12},{9,13},{10,... | collective-permute-start | bytes 516104 | tf_op jit(solution)/shard_map/ppermute | solution.py:26
  120.7 9.3 %collective-permute-start.14 = (bf16[84,1024]{1,0:T(8,128)(2,1)S(1)}, bf16[84,1024]{1,0:T(8,128)(2,1)S(1)}, u32[]{:S(2)}, u32[]{:S(2)}) collective-permute-start(bf16[84,1024]{1,0:T(8,128)(2,1)S(1)} %constant_dynamic-slice_fusion.12), channel_id=1, source_target_pairs={{0,8},{8,0},{16,24},{24,16},{1,9},{9,1},{17,25},{25,17},{2,10},{10... | collective-permute-start | bytes 516104 | tf_op jit(solution)/shard_map/ppermute | solution.py:26
  122.2 14.2 %collective-permute-start.24 = (bf16[88,1024]{1,0:T(8,128)(2,1)S(1)}, bf16[88,1024]{1,0:T(8,128)(2,1)S(1)}, u32[]{:S(2)}, u32[]{:S(2)}) collective-permute-start(bf16[88,1024]{1,0:T(8,128)(2,1)S(1)} %constant_dynamic-slice_fusion.7), channel_id=1, source_target_pairs={{0,16},{8,24},{16,0},{24,8},{1,17},{9,25},{17,1},{25,9},{2,18},{10... | collective-permute-start | bytes 540680 | tf_op jit(solution)/shard_map/ppermute | solution.py:26
  125.0 11.6 %collective-permute-start.5 = (bf16[42,1024]{1,0:T(8,128)(2,1)S(1)}, bf16[42,1024]{1,0:T(8,128)(2,1)S(1)}, u32[]{:S(2)}, u32[]{:S(2)}) collective-permute-start(bf16[42,1024]{1,0:T(8,128)(2,1)S(1)} %constant_dynamic-slice_fusion.16), channel_id=1, source_target_pairs={{0,8},{8,0},{16,24},{24,16},{1,9},{9,1},{17,25},{25,17},{2,10},{10... | collective-permute-start | bytes 258056 | tf_op jit(solution)/shard_map/ppermute | solution.py:26
  130.2 7.4 %collective-permute-start.15 = (bf16[42,1024]{1,0:T(8,128)(2,1)S(1)}, bf16[42,1024]{1,0:T(8,128)(2,1)S(1)}, u32[]{:S(2)}, u32[]{:S(2)}) collective-permute-start(bf16[42,1024]{1,0:T(8,128)(2,1)S(1)} %constant_dynamic-slice_fusion.11), channel_id=1, source_target_pairs={{0,16},{8,24},{16,0},{24,8},{1,17},{9,25},{17,1},{25,9},{2,18},{10... | collective-permute-start | bytes 258056 | tf_op jit(solution)/shard_map/ppermute | solution.py:26
  136.5 7.5 %collective-permute-start.25 = (bf16[44,1024]{1,0:T(8,128)(2,1)S(1)}, bf16[44,1024]{1,0:T(8,128)(2,1)S(1)}, u32[]{:S(2)}, u32[]{:S(2)}) collective-permute-start(bf16[44,1024]{1,0:T(8,128)(2,1)S(1)} %constant_dynamic-slice_fusion.6), channel_id=1, source_target_pairs={{0,2},{1,3},{2,0},{3,1},{4,6},{5,7},{6,4},{7,5},{8,10},{9,11},{10,... | collective-permute-start | bytes 270344 | tf_op jit(solution)/shard_map/ppermute | solution.py:26
  136.7 5.4 %collective-permute-start.6 = (bf16[21,1024]{1,0:T(8,128)(2,1)S(1)}, bf16[21,1024]{1,0:T(8,128)(2,1)S(1)}, u32[]{:S(2)}, u32[]{:S(2)}) collective-permute-start(bf16[21,1024]{1,0:T(8,128)(2,1)S(1)} %constant_dynamic-slice_fusion.15), channel_id=1, source_target_pairs={{0,16},{8,24},{16,0},{24,8},{1,17},{9,25},{17,1},{25,9},{2,18},{10... | collective-permute-start | bytes 129032 | tf_op jit(solution)/shard_map/ppermute | solution.py:26
  137.7 4.5 %collective-permute-start.16 = (bf16[21,1024]{1,0:T(8,128)(2,1)S(1)}, bf16[21,1024]{1,0:T(8,128)(2,1)S(1)}, u32[]{:S(2)}, u32[]{:S(2)}) collective-permute-start(bf16[21,1024]{1,0:T(8,128)(2,1)S(1)} %constant_dynamic-slice_fusion.10), channel_id=1, source_target_pairs={{0,2},{1,3},{2,0},{3,1},{4,6},{5,7},{6,4},{7,5},{8,10},{9,11},{10,... | collective-permute-start | bytes 129032 | tf_op jit(solution)/shard_map/ppermute | solution.py:26
  142.1 6.7 %collective-permute-start.7 = (bf16[21,1024]{1,0:T(8,128)(2,1)S(1)}, bf16[21,1024]{1,0:T(8,128)(2,1)S(1)}, u32[]{:S(2)}, u32[]{:S(2)}) collective-permute-start(bf16[21,1024]{1,0:T(8,128)(2,1)S(1)} %add_convert_fusion.18), channel_id=1, source_target_pairs={{0,16},{8,24},{16,0},{24,8},{1,17},{9,25},{17,1},{25,9},{2,18},{10... | collective-permute-start | bytes 129032 | tf_op jit(solution)/shard_map/ppermute | solution.py:26
  142.3 6.7 %collective-permute-start.17 = (bf16[21,1024]{1,0:T(8,128)(2,1)S(1)}, bf16[21,1024]{1,0:T(8,128)(2,1)S(1)}, u32[]{:S(2)}, u32[]{:S(2)}) collective-permute-start(bf16[21,1024]{1,0:T(8,128)(2,1)S(1)} %add_convert_fusion.17), channel_id=1, source_target_pairs={{0,2},{1,3},{2,0},{3,1},{4,6},{5,7},{6,4},{7,5},{8,10},{9,11},{10,... | collective-permute-start | bytes 129032 | tf_op jit(solution)/shard_map/ppermute | solution.py:26
  144.1 4.9 %collective-permute-start.26 = (bf16[22,1024]{1,0:T(8,128)(2,1)S(1)}, bf16[22,1024]{1,0:T(8,128)(2,1)S(1)}, u32[]{:S(2)}, u32[]{:S(2)}) collective-permute-start(bf16[22,1024]{1,0:T(8,128)(2,1)S(1)} %constant_dynamic-slice_fusion.5), channel_id=1, source_target_pairs={{0,4},{1,5},{2,6},{3,7},{4,0},{5,1},{6,2},{7,3},{8,12},{9,13},{10,... | collective-permute-start | bytes 135176 | tf_op jit(solution)/shard_map/ppermute | solution.py:26
  148.9 7.9 %collective-permute-start.8 = (bf16[42,1024]{1,0:T(8,128)(2,1)S(1)}, bf16[42,1024]{1,0:T(8,128)(2,1)S(1)}, u32[]{:S(2)}, u32[]{:S(2)}) collective-permute-start(bf16[42,1024]{1,0:T(8,128)(2,1)S(1)} %pad_maximum_fusion.10), channel_id=1, source_target_pairs={{0,8},{8,0},{16,24},{24,16},{1,9},{9,1},{17,25},{25,17},{2,10},{10... | collective-permute-start | bytes 258056 | tf_op jit(solution)/shard_map/ppermute | solution.py:26
  149.0 4.2 %collective-permute-start.27 = (bf16[22,1024]{1,0:T(8,128)(2,1)S(1)}, bf16[22,1024]{1,0:T(8,128)(2,1)S(1)}, u32[]{:S(2)}, u32[]{:S(2)}) collective-permute-start(bf16[22,1024]{1,0:T(8,128)(2,1)S(1)} %add_convert_fusion.16), channel_id=1, source_target_pairs={{0,4},{1,5},{2,6},{3,7},{4,0},{5,1},{6,2},{7,3},{8,12},{9,13},{10,... | collective-permute-start | bytes 135176 | tf_op jit(solution)/shard_map/ppermute | solution.py:26
  149.2 9.6 %collective-permute-start.18 = (bf16[42,1024]{1,0:T(8,128)(2,1)S(1)}, bf16[42,1024]{1,0:T(8,128)(2,1)S(1)}, u32[]{:S(2)}, u32[]{:S(2)}) collective-permute-start(bf16[42,1024]{1,0:T(8,128)(2,1)S(1)} %pad_maximum_fusion.11), channel_id=1, source_target_pairs={{0,16},{8,24},{16,0},{24,8},{1,17},{9,25},{17,1},{25,9},{2,18},{10... | collective-permute-start | bytes 258056 | tf_op jit(solution)/shard_map/ppermute | solution.py:26
  153.2 5.8 %collective-permute-start.28 = (bf16[44,1024]{1,0:T(8,128)(2,1)S(1)}, bf16[44,1024]{1,0:T(8,128)(2,1)S(1)}, u32[]{:S(2)}, u32[]{:S(2)}) collective-permute-start(bf16[44,1024]{1,0:T(8,128)(2,1)S(1)} %pad_maximum_fusion.12), channel_id=1, source_target_pairs={{0,2},{1,3},{2,0},{3,1},{4,6},{5,7},{6,4},{7,5},{8,10},{9,11},{10,... | collective-permute-start | bytes 270344 | tf_op jit(solution)/shard_map/ppermute | solution.py:26
  156.9 7.4 %collective-permute-start.9 = (bf16[84,1024]{1,0:T(8,128)(2,1)S(1)}, bf16[84,1024]{1,0:T(8,128)(2,1)S(1)}, u32[]{:S(2)}, u32[]{:S(2)}) collective-permute-start(bf16[84,1024]{1,0:T(8,128)(2,1)S(1)} %pad_maximum_fusion.7), channel_id=1, source_target_pairs={{0,4},{1,5},{2,6},{3,7},{4,0},{5,1},{6,2},{7,3},{8,12},{9,13},{10,... | collective-permute-start | bytes 516104 | tf_op jit(solution)/shard_map/ppermute | solution.py:26
  158.9 9.4 %collective-permute-start.19 = (bf16[84,1024]{1,0:T(8,128)(2,1)S(1)}, bf16[84,1024]{1,0:T(8,128)(2,1)S(1)}, u32[]{:S(2)}, u32[]{:S(2)}) collective-permute-start(bf16[84,1024]{1,0:T(8,128)(2,1)S(1)} %pad_maximum_fusion.8), channel_id=1, source_target_pairs={{0,8},{8,0},{16,24},{24,16},{1,9},{9,1},{17,25},{25,17},{2,10},{10... | collective-permute-start | bytes 516104 | tf_op jit(solution)/shard_map/ppermute | solution.py:26
  159.1 10.2 %collective-permute-start.29 = (bf16[88,1024]{1,0:T(8,128)(2,1)S(1)}, bf16[88,1024]{1,0:T(8,128)(2,1)S(1)}, u32[]{:S(2)}, u32[]{:S(2)}) collective-permute-start(bf16[88,1024]{1,0:T(8,128)(2,1)S(1)} %pad_maximum_fusion.9), channel_id=1, source_target_pairs={{0,16},{8,24},{16,0},{24,8},{1,17},{9,25},{17,1},{25,9},{2,18},{10... | collective-permute-start | bytes 540680 | tf_op jit(solution)/shard_map/ppermute | solution.py:26
  164.5 7.3 %collective-permute-start.10 = (bf16[168,1024]{1,0:T(8,128)(2,1)S(1)}, bf16[168,1024]{1,0:T(8,128)(2,1)S(1)}, u32[]{:S(2)}, u32[]{:S(2)}) collective-permute-start(bf16[168,1024]{1,0:T(8,128)(2,1)S(1)} %pad_maximum_fusion.4), channel_id=1, source_target_pairs={{0,2},{1,3},{2,0},{3,1},{4,6},{5,7},{6,4},{7,5},{8,10},{9,11},{10,... | collective-permute-start | bytes 1032200 | tf_op jit(solution)/shard_map/ppermute | solution.py:26
  168.4 7.3 %collective-permute-start.20 = (bf16[168,1024]{1,0:T(8,128)(2,1)S(1)}, bf16[168,1024]{1,0:T(8,128)(2,1)S(1)}, u32[]{:S(2)}, u32[]{:S(2)}) collective-permute-start(bf16[168,1024]{1,0:T(8,128)(2,1)S(1)} %pad_maximum_fusion.5), channel_id=1, source_target_pairs={{0,4},{1,5},{2,6},{3,7},{4,0},{5,1},{6,2},{7,3},{8,12},{9,13},{10,... | collective-permute-start | bytes 1032200 | tf_op jit(solution)/shard_map/ppermute | solution.py:26
  169.5 7.5 %collective-permute-start.30 = (bf16[176,1024]{1,0:T(8,128)(2,1)S(1)}, bf16[176,1024]{1,0:T(8,128)(2,1)S(1)}, u32[]{:S(2)}, u32[]{:S(2)}) collective-permute-start(bf16[176,1024]{1,0:T(8,128)(2,1)S(1)} %pad_maximum_fusion.3), channel_id=1, source_target_pairs={{0,8},{8,0},{16,24},{24,16},{1,9},{9,1},{17,25},{25,17},{2,10},{10... | collective-permute-start | bytes 1081352 | tf_op jit(solution)/shard_map/ppermute | solution.py:26
  172.0 5.3 %collective-permute-start.11 = (bf16[336,1024]{1,0:T(8,128)(2,1)S(1)}, bf16[336,1024]{1,0:T(8,128)(2,1)S(1)}, u32[]{:S(2)}, u32[]{:S(2)}) collective-permute-start(bf16[336,1024]{1,0:T(8,128)(2,1)S(1)} %pad_maximum_fusion.1), channel_id=1, source_target_pairs={{0,1},{1,0},{2,3},{3,2},{4,5},{5,4},{6,7},{7,6},{8,9},{9,8},{10,11... | collective-permute-start | bytes 2064392 | tf_op jit(solution)/shard_map/ppermute | solution.py:26
  175.9 2.2 %collective-permute-start.21 = (bf16[336,1024]{1,0:T(8,128)(2,1)S(1)}, bf16[336,1024]{1,0:T(8,128)(2,1)S(1)}, u32[]{:S(2)}, u32[]{:S(2)}) collective-permute-start(bf16[336,1024]{1,0:T(8,128)(2,1)S(1)} %pad_maximum_fusion.2), channel_id=1, source_target_pairs={{0,1},{1,0},{2,3},{3,2},{4,5},{5,4},{6,7},{7,6},{8,9},{9,8},{10,11... | collective-permute-start | bytes 2064392 | tf_op jit(solution)/shard_map/ppermute | solution.py:26
  177.2 2.3 %collective-permute-start.31 = (bf16[352,1024]{1,0:T(8,128)(2,1)S(1)}, bf16[352,1024]{1,0:T(8,128)(2,1)S(1)}, u32[]{:S(2)}, u32[]{:S(2)}) collective-permute-start(bf16[352,1024]{1,0:T(8,128)(2,1)S(1)} %pad_maximum_fusion), channel_id=1, source_target_pairs={{0,1},{1,0},{2,3},{3,2},{4,5},{5,4},{6,7},{7,6},{8,9},{9,8},{10,11... | collective-permute-start | bytes 2162696 | tf_op jit(solution)/shard_map/ppermute | solution.py:26
  (25 other events, 64.7 us)

commit v3 on v2

--- a/solution.py
+++ b/solution.py
@@ -159,8 +159,14 @@
     slots = trainers * CAP
     core, low, high, feat = links()
     weights = jnp.concatenate([first_root, first_near], axis=0)
-    for link in feat:
-        weights = gather_step(weights, link)
+    place, depth = lax.axis_index("feat"), weights.shape[0]
+    gathered = jnp.zeros((feat_size * depth, weights.shape[1]), weights.dtype)
+    for shift in range(feat_size):
+        pairs = [(i, (i + shift) % feat_size) for i in range(feat_size)]
+        piece = lax.ppermute(weights, "feat", pairs) if shift else weights
+        source = (place - shift + feat_size) % feat_size
+        gathered = lax.dynamic_update_slice_in_dim(gathered, piece, source * depth, 0)
+    weights = gathered
     node_ids = jnp.arange(node_count, dtype=jnp.int32)
     earlier = (owner_map[:, None] == owner_map[None, :]) & (node_ids[:, None] < node_ids[None, :])
     slot_rank = jnp.sum(earlier.astype(jnp.int32), axis=0)
@@ -208,13 +214,6 @@
     )
     both = jnp.concatenate([root_rows, near_two], axis=1)
     grad_two = cross_rows(both, slope_two).astype(jnp.bfloat16)
-    units = grad_two.shape[0] // owners_all
-    ends = [(units * part // 3) * owners_all for part in range(4)]
-    grad_two = sum_parts(
-        [grad_two[ends[part] : ends[part + 1]] for part in range(3)],
-        [core + low + high + feat, core + high + feat + low, core + feat + low + high],
-    )
-    grad_two = jnp.concatenate(grad_two, axis=0)
     back_root = cross_cols(slope_two, second_root).astype(jnp.bfloat16)
     back_near = (cross_cols(slope_two, second_near) / divisor).astype(jnp.bfloat16)
     table_grad = cross_rows(root_pick, back_root) + cross_rows(multiples, back_near)
@@ -223,22 +222,34 @@
     )
     grad_one = jnp.dot(arrived, pre_grad, preferred_element_type=jnp.float32)
     grad_one = grad_one.astype(jnp.bfloat16)
-    for link in reversed(feat):
-        grad_one = scatter_step(grad_one, link)
-    (grad_one,) = sum_parts([grad_one], [core + low + high])
-    grad_one = grad_one.reshape(2, block_width, -1)
     biases = jnp.stack(
         [
             jnp.sum(slope_two.astype(jnp.float32), axis=0),
             jnp.sum(pre_grad.astype(jnp.float32), axis=0),
         ]
     )
-    for link in core + low + high + feat:
-        biases = biases + exchange(biases, link)
-    biasgrad_two, biasgrad_one = biases
-    grad_two = grad_two.astype(jnp.float32).reshape(2, -1, grad_two.shape[1])
-    rootgrad_two, neargrad_two = grad_two
-    rootgrad_one, neargrad_one = grad_one.astype(jnp.float32)
+    rows_two, rows_one = grad_two.shape[0], grad_one.shape[0]
+    units = -(-(rows_two + rows_one + 2) // owners_all)
+    padding = units * owners_all - rows_two - rows_one
+    biases = jnp.pad(biases.astype(jnp.bfloat16), ((0, padding - 2), (0, 0)))
+    one, two = (units // 3) * owners_all, (2 * units // 3) * owners_all
+    last = jnp.concatenate([grad_two[two:], grad_one, biases], axis=0)
+    total = jnp.concatenate(
+        sum_parts(
+            [grad_two[:one], grad_two[one:two], last],
+            [core + low + high + feat, core + high + feat + low, core + feat + low + high],
+        ),
+        axis=0,
+    )
+    half = rows_two // 2
+    rootgrad_two = total[:half].astype(jnp.float32)
+    neargrad_two = total[half:rows_two].astype(jnp.float32)
+    grad_one = lax.dynamic_slice_in_dim(
+        total[rows_two : rows_two + rows_one], place * depth, depth, 0
+    ).astype(jnp.float32)
+    rootgrad_one, neargrad_one = grad_one[:block_width], grad_one[block_width:]
+    biasgrad_two = total[rows_two + rows_one].astype(jnp.float32)
+    biasgrad_one = total[rows_two + rows_one + 1].astype(jnp.float32)
     return (
         layer_output,
         rootgrad_two,

time: 185 us -> 156 us (0.84)
  waiting for transfers between devices: 75.3 us -> 43.2 us
  other arithmetic: 10.7 us -> 22.3 us
  starting transfers between devices: 46 us -> 37.6 us
    ppermute x45 -> x30, waiting for transfers between devices: 67.9 us -> 38.6 us  [exchange(): return lax.ppermute(rows, axis, pairs)]
    ppermute x45 -> x30, starting transfers between devices: 41.2 us -> 27.7 us  [exchange(): return lax.ppermute(rows, axis, pairs)]
    ppermute x0 -> x3, starting transfers between devices: none -> 6.96 us  [local(): piece = lax.ppermute(weights, 'feat', pairs) if shift else weights]
    another operation x3 -> x2, local copies, waits for them, and re-layouts: 5.75 us -> 0.01 us  [local(): jnp.stack([jnp.sum(slope_two.astype(jnp.float32), axis=0), jnp.sum(pre_gr...]
    convert_element_type x1 -> x3, other arithmetic: 0.02 us -> 4.48 us  [the longest x1 3.84 us: local(): neargrad_two = total[half:rows_two].astype(jnp.float32)]
    convert_element_type x20 -> x15, other arithmetic: 1.62 us -> 5.33 us  [scatter_step(): (kept.astype(jnp.float32) + got.astype(jnp.float32)).astype(jnp.bfloat16)]
    all_to_all x1, waiting for transfers between devices: 7.37 us -> 4.61 us  [local(): lax.all_to_all(packed, ('feat', 'trainer'), split_axis=1, concat_axis=1,...]
    dynamic_update_slice x0 -> x4, local copies, waits for them, and re-layouts: none -> 2.66 us  [local(): lax.dynamic_update_slice_in_dim(gathered, piece, source * depth, 0)]
  transfers between devices with their start and end apart: 46 -> 34, of which waited for: 31 -> 16; matrix products, arithmetic and copies ran while one was open for 12% -> 16% of each run, Pallas kernels for 7% -> 8%
where the time goes in v3:
time: 156 us
  waiting for transfers between devices  43.2 us (28%)
  starting transfers between devices  37.6 us (24%)
  matrix products  24.3 us (16%)
  other arithmetic  22.3 us (14%)
  local copies, waits for them, and re-layouts  14.3 us (9%)
  Pallas kernels  12.4 us (8%)
    ppermute x30, waiting for transfers between devices, exchange(): return lax.ppermute(rows, axis, pairs)  38.6 us
    ppermute x30, starting transfers between devices, exchange(): return lax.ppermute(rows, axis, pairs)  27.7 us
    dot_general x4, matrix products, cross_rows(): lax.dot_general(left, right, (((0,), (0,)), ((), ())), preferred_element_...  15.6 us
    pallas_call x1, Pallas kernels, select(): pl.pallas_call(functools.partial(select_kernel, fanout), grid=(steps,), i...  12.4 us
    ppermute x3, starting transfers between devices, local(): piece = lax.ppermute(weights, 'feat', pairs) if shift else weights  6.96 us
    convert_element_type x15, other arithmetic, scatter_step(): (kept.astype(jnp.float32) + got.astype(jnp.float32)).astype(jnp.bfloat16)  5.33 us
    all_to_all x1, waiting for transfers between devices, local(): lax.all_to_all(packed, ('feat', 'trainer'), split_axis=1, concat_axis=1,...  4.61 us
    convert_element_type x1, other arithmetic, local(): neargrad_two = total[half:rows_two].astype(jnp.float32)  3.84 us
  transfers between devices with their start and end apart: 34, of which 16 were waited for; matrix products, arithmetic and copies ran while one was open for 16% of the time, Pallas kernels for 8%

profile of v3, /device:TPU:0, one launch (start us, length us, event | category | flops | bytes accessed | tf_op | source)
XLA Modules:
  0.0 155.6 jit_solution(11629767844089671159)
XLA Ops:
  0.6 1.0 constant_dynamic-update-slice_fusion.5
  2.5 3.0 %collective-permute-start = (bf16[64,1024]{1,0:T(8,128)(2,1)S(1)}, bf16[64,1024]{1,0:T(8,128)(2,1)S(1)}, u32[]{:S(2)}, u32[]{:S(2)}) collective-permute-start(bf16[64,1024]{1,0:T(8,128)(2,1)S(1)} %constant_dynamic-update-slice_fusion.4), channel_id=1, source_target_pairs={{0,8},{8,16},{16,24},{24,0},{1,9},{9,17},{17,25},{25,1},{2,10},{10... | collective-permute-start | bytes 393224 | tf_op jit(solution)/shard_map/ppermute | solution.py:166
  5.5 2.6 %collective-permute-start.1 = (bf16[64,1024]{1,0:T(8,128)(2,1)S(1)}, bf16[64,1024]{1,0:T(8,128)(2,1)S(1)}, u32[]{:S(2)}, u32[]{:S(2)}) collective-permute-start(bf16[64,1024]{1,0:T(8,128)(2,1)S(1)} %constant_dynamic-update-slice_fusion.4), channel_id=1, source_target_pairs={{0,16},{8,24},{16,0},{24,8},{1,17},{9,25},{17,1},{25,9},{2,18},{10... | collective-permute-start | bytes 393224 | tf_op jit(solution)/shard_map/ppermute | solution.py:166
  8.1 1.3 collective-permute-start.2
  10.9 1.3 add_bitcast_fusion.ids_ref
  12.2 12.4 %shard_map.198 = f32[32,1024]{1,0:T(8,128)} custom-call(s32[16,512]{1,0:T(8,128)} %add_bitcast_fusion.ids_ref, bf16[32,4096]{1,0:T(8,128)(2,1)} %feat_ref.1), custom_call_target="tpu_custom_call" | custom-call | flops 2684354560 | bytes 262144 | tf_op jit(solution)/shard_map/pallas_call | solution.py:106
  24.6 1.0 reshape.50
  27.6 2.9 %all-to-all-start = ((bf16[32,2,1024]{2,1,0:T(2,128)(2,1)}), bf16[32,2,1024]{2,1,0:T(2,128)(2,1)S(1)}, u32[]{:S(2)}, u32[]{:S(2)}) async-start(bf16[32,2,1024]{2,1,0:T(2,128)(2,1)} %reshape.56), calls=%async_computation | async-start | bytes 262144 | tf_op jit(solution)/shard_map/all_to_all | solution.py:182
  34.1 4.6 %all-to-all-done = bf16[32,2,1024]{2,1,0:T(2,128)(2,1)S(1)} async-done(((bf16[32,2,1024]{2,1,0:T(2,128)(2,1)}), bf16[32,2,1024]{2,1,0:T(2,128)(2,1)S(1)}, u32[]{:S(2)}, u32[]{:S(2)}) %all-to-all-start) | async-done | bytes 131104 | tf_op jit(solution)/shard_map/all_to_all | solution.py:182
  40.1 2.0 %fusion.10 = bf16[256,1024]{1,0:T(8,128)(2,1)S(1)} fusion(bf16[256,256]{1,0:T(8,128)(2,1)S(1)} %reshape.53, bf16[256,1024]{1,0:T(8,128)(2,1)} %constant_dynamic-update-slice_fusion, f32[1024]{0:T(1024)S(1)} %copy-done.12), kind=kOutput, calls=%fused_computation.33 | convolution fusion | flops 136314880 | bytes 1183744 | tf_op jit(solution)/shard_map/dot_general | solution.py:125
  42.6 1.3 fusion.42
  43.9 3.5 %divide_convert_fusion.1 = bf16[512,1024]{1,0:T(8,128)(2,1)S(1)} fusion(bf16[256,1024]{1,0:T(8,128)(2,1)S(1)} %fusion.10, f32[512]{0:T(512)S(1)} %convert_element_type.233, s32[512]{0:T(512)S(1)} %bitcast.68, s32[512]{0:T(512)S(1)} %bitcast.70, s32[512]{0:T(512)S(1)} %bitcast.54, s32[512]{0:T(512)S(1)} %bitcast.56, s32[512]{0:T(512)S(1)} %bitcast.58, ...), kind=kOutput, calls=%fused_computation.17 | convolution fusion | flops 274726912 | bytes 1600512 | tf_op jit(solution)/shard_map/dot_general | solution.py:204
  47.5 2.6 %multiply_convert_fusion.1 = (bf16[512,1024]{1,0:T(8,128)(2,1)}, f32[512,1024]{1,0:T(8,128)S(1)}) fusion(f32[1024]{0:T(1024)S(1)} %copy-done.13, f32[512,1024]{1,0:T(8,128)S(1)} %fusion.42, bf16[512,1024]{1,0:T(8,128)(2,1)S(1)} %divide_convert_fusion.1, bf16[1024,1024]{1,0:T(8,128)(2,1)S(1)} %copy-done), kind=kOutput, calls=%fused_computation.14 | convolution fusion | flops 1077411840 | bytes 8392704 | tf_op jit(solution)/shard_map/dot_general | solution.py:208
  50.1 1.9 %fusion.37 = (bf16[1024]{0:T(1024)(128)(2,1)S(1)}, bf16[512,1024]{1,0:T(8,128)(2,1)}) fusion(f32[512,1024]{1,0:T(8,128)S(1)} %get-tuple-element.68, bf16[512,1024]{1,0:T(8,128)(2,1)S(1)} %copy-done.4), kind=kLoop, calls=%fused_computation.168 | loop fusion | flops 5766144 | bytes 4196352 | tf_op jit(solution)/shard_map/reduce_sum | solution.py:227
  52.0 4.4 %fusion.8 = f32[256,1024]{1,0:T(8,128)} fusion(bf16[512,1024]{1,0:T(8,128)(2,1)} %get-tuple-element.8, bf16[1024,1024]{1,0:T(8,128)(2,1)S(1)} %copy-done, f32[512]{0:T(512)S(1)} %convert_element_type.233, s32[512]{0:T(512)S(1)} %bitcast.69, s32[512]{0:T(512)S(1)} %bitcast.71, s32[512]{0:T(512)S(1)} %bitcast.55, s32[512]{0:T(512)S(1)} %bitcast.57, ...), kind=kOutput, calls=%fused_computation.31 | convolution fusion | flops 1348468736 | bytes 4221952 | tf_op jit(solution)/shard_map/dot_general | solution.py:125
  56.3 3.9 %convolution_convert_fusion = bf16[2048,1024]{1,0:T(8,128)(2,1)S(1)} fusion(bf16[512,1024]{1,0:T(8,128)(2,1)} %get-tuple-element.8, bf16[512,1024]{1,0:T(8,128)(2,1)} %copy-done.14, bf16[512,1024]{1,0:T(8,128)(2,1)S(1)} %convolution_convert_fusion.2), kind=kOutput, calls=%fused_computation | convolution fusion | flops 2153775104 | bytes 7340032 | tf_op jit(solution)/shard_map/dot_general | solution.py:125
  60.3 1.1 slice.95
  61.7 5.4 %fusion.41 = (bf16[1024]{0:T(1024)(128)(2,1)S(1)}, bf16[256,1024]{1,0:T(8,128)(2,1)}) fusion(bf16[256,1024]{1,0:T(8,128)(2,1)} %copy-done.5, f32[256,1024]{1,0:T(8,128)} %fusion.8, bf16[512,1024]{1,0:T(8,128)(2,1)} %get-tuple-element.8, bf16[1024,1024]{1,0:T(8,128)(2,1)} %param.26, s32[512]{0:T(512)S(1)} %copy-done.10), kind=kOutput, calls=%fused_computation.172 | convolution fusion | flops 1344666624 | bytes 5246976 | tf_op jit(solution)/shard_map/dot_general | solution.py:125
  67.1 1.0 constant_dynamic-slice_fusion.9
  71.1 1.7 %add_convert_fusion.1 = bf16[384,1024]{1,0:T(8,128)(2,1)S(1)} fusion(bf16[384,1024]{1,0:T(8,128)(2,1)} %collective-permute-done.13, bf16[768,1024]{1,0:T(8,128)(2,1)} %copy-done.2, s32[]{:T(128)S(6)} %select_n.352), kind=kLoop, calls=%fused_computation.22 | loop fusion | flops 1572864 | bytes 2359300 | tf_op jit(solution)/shard_map/convert_element_type | solution.py:39
  73.4 1.4 add_convert_fusion.2
  75.7 1.5 add_convert_fusion
  78.0 6.3 %collective-permute-done.14 = bf16[192,1024]{1,0:T(8,128)(2,1)S(1)} collective-permute-done((bf16[192,1024]{1,0:T(8,128)(2,1)S(1)}, bf16[192,1024]{1,0:T(8,128)(2,1)S(1)}, u32[]{:S(2)}, u32[]{:S(2)}) %collective-permute-start.14) | collective-permute-done | bytes 393248 | tf_op jit(solution)/shard_map/ppermute | solution.py:26
  85.1 1.0 collective-permute-done.4
  86.3 1.4 collective-permute-start.5
  87.8 1.8 %collective-permute-done.24 = bf16[200,1024]{1,0:T(8,128)(2,1)S(1)} collective-permute-done((bf16[200,1024]{1,0:T(8,128)(2,1)S(1)}, bf16[200,1024]{1,0:T(8,128)(2,1)S(1)}, u32[]{:S(2)}, u32[]{:S(2)}) %collective-permute-start.24) | collective-permute-done | bytes 409632 | tf_op jit(solution)/shard_map/ppermute | solution.py:26
  90.4 3.8 %collective-permute-done.15 = bf16[96,1024]{1,0:T(8,128)(2,1)S(1)} collective-permute-done((bf16[96,1024]{1,0:T(8,128)(2,1)S(1)}, bf16[96,1024]{1,0:T(8,128)(2,1)S(1)}, u32[]{:S(2)}, u32[]{:S(2)}) %collective-permute-start.15) | collective-permute-done | bytes 196640 | tf_op jit(solution)/shard_map/ppermute | solution.py:26
  95.1 2.5 %collective-permute-start.6 = (bf16[48,1024]{1,0:T(8,128)(2,1)S(1)}, bf16[48,1024]{1,0:T(8,128)(2,1)S(1)}, u32[]{:S(2)}, u32[]{:S(2)}) collective-permute-start(bf16[48,1024]{1,0:T(8,128)(2,1)S(1)} %constant_dynamic-slice_fusion.11), channel_id=1, source_target_pairs={{0,8},{8,0},{16,24},{24,16},{1,9},{9,1},{17,25},{25,17},{2,10},{10... | collective-permute-start | bytes 294920 | tf_op jit(solution)/shard_map/ppermute | solution.py:26
  97.6 6.3 %collective-permute-done.25 = bf16[100,1024]{1,0:T(8,128)(2,1)S(1)} collective-permute-done((bf16[100,1024]{1,0:T(8,128)(2,1)S(1)}, bf16[100,1024]{1,0:T(8,128)(2,1)S(1)}, u32[]{:S(2)}, u32[]{:S(2)}) %collective-permute-start.25) | collective-permute-done | bytes 204832 | tf_op jit(solution)/shard_map/ppermute | solution.py:26
  104.0 1.2 collective-permute-start.26
  105.2 1.2 collective-permute-start.17
  106.5 3.3 %collective-permute-done.17 = bf16[24,1024]{1,0:T(8,128)(2,1)S(1)} collective-permute-done((bf16[24,1024]{1,0:T(8,128)(2,1)S(1)}, bf16[24,1024]{1,0:T(8,128)(2,1)S(1)}, u32[]{:S(2)}, u32[]{:S(2)}) %collective-permute-start.17) | collective-permute-done | bytes 49184 | tf_op jit(solution)/shard_map/ppermute | solution.py:26
  110.6 1.4 collective-permute-done.7
  112.2 1.2 collective-permute-start.27
  114.1 2.4 %collective-permute-start.19 = (bf16[48,1024]{1,0:T(8,128)(2,1)S(1)}, bf16[48,1024]{1,0:T(8,128)(2,1)S(1)}, u32[]{:S(2)}, u32[]{:S(2)}) collective-permute-start(bf16[48,1024]{1,0:T(8,128)(2,1)S(1)} %pad_maximum_fusion.17), channel_id=1, source_target_pairs={{0,16},{8,24},{16,0},{24,8},{1,17},{9,25},{17,1},{25,9},{2,18},{10... | collective-permute-start | bytes 294920 | tf_op jit(solution)/shard_map/ppermute | solution.py:26
  117.2 1.2 collective-permute-start.28
  118.5 1.6 %collective-permute-start.9 = (bf16[48,1024]{1,0:T(8,128)(2,1)S(1)}, bf16[48,1024]{1,0:T(8,128)(2,1)S(1)}, u32[]{:S(2)}, u32[]{:S(2)}) collective-permute-start(bf16[48,1024]{1,0:T(8,128)(2,1)S(1)} %pad_maximum_fusion.16), channel_id=1, source_target_pairs={{0,8},{8,0},{16,24},{24,16},{1,9},{9,1},{17,25},{25,17},{2,10},{10... | collective-permute-start | bytes 294920 | tf_op jit(solution)/shard_map/ppermute | solution.py:26
  120.1 2.1 %collective-permute-done.28 = bf16[25,1024]{1,0:T(8,128)(2,1)S(1)} collective-permute-done((bf16[25,1024]{1,0:T(8,128)(2,1)S(1)}, bf16[25,1024]{1,0:T(8,128)(2,1)S(1)}, u32[]{:S(2)}, u32[]{:S(2)}) %collective-permute-start.28) | collective-permute-done | bytes 51232 | tf_op jit(solution)/shard_map/ppermute | solution.py:26
  123.3 1.5 collective-permute-start.20
  124.8 1.5 collective-permute-start.10
  126.3 2.1 %collective-permute-done.29 = bf16[50,1024]{1,0:T(8,128)(2,1)S(1)} collective-permute-done((bf16[50,1024]{1,0:T(8,128)(2,1)S(1)}, bf16[50,1024]{1,0:T(8,128)(2,1)S(1)}, u32[]{:S(2)}, u32[]{:S(2)}) %collective-permute-start.29) | collective-permute-done | bytes 102432 | tf_op jit(solution)/shard_map/ppermute | solution.py:26
  128.4 2.4 %collective-permute-start.30 = (bf16[100,1024]{1,0:T(8,128)(2,1)S(1)}, bf16[100,1024]{1,0:T(8,128)(2,1)S(1)}, u32[]{:S(2)}, u32[]{:S(2)}) collective-permute-start(bf16[100,1024]{1,0:T(8,128)(2,1)S(1)} %pad_maximum_fusion.12), channel_id=1, source_target_pairs={{0,16},{8,24},{16,0},{24,8},{1,17},{9,25},{17,1},{25,9},{2,18},{10... | collective-permute-start | bytes 614408 | tf_op jit(solution)/shard_map/ppermute | solution.py:26
  130.9 1.2 collective-permute-start.21
  133.2 4.3 %collective-permute-done.30 = bf16[100,1024]{1,0:T(8,128)(2,1)S(1)} collective-permute-done((bf16[100,1024]{1,0:T(8,128)(2,1)S(1)}, bf16[100,1024]{1,0:T(8,128)(2,1)S(1)}, u32[]{:S(2)}, u32[]{:S(2)}) %collective-permute-start.30) | collective-permute-done | bytes 204832 | tf_op jit(solution)/shard_map/ppermute | solution.py:26
  141.6 4.1 %collective-permute-done.31 = bf16[200,1024]{1,0:T(8,128)(2,1)S(1)} collective-permute-done((bf16[200,1024]{1,0:T(8,128)(2,1)S(1)}, bf16[200,1024]{1,0:T(8,128)(2,1)S(1)}, u32[]{:S(2)}, u32[]{:S(2)}) %collective-permute-start.31) | collective-permute-done | bytes 409632 | tf_op jit(solution)/shard_map/ppermute | solution.py:26
  146.8 1.5 broadcast_select_fusion.2
  148.4 1.5 broadcast_select_fusion.5
  151.8 3.8 %fusion = (f32[1024,1024]{1,0:T(8,128)}, f32[1024,1024]{1,0:T(8,128)}) fusion(bf16[400,1024]{1,0:T(8,128)(2,1)S(1)} %get-tuple-element.12, bf16[400,1024]{1,0:T(8,128)(2,1)S(1)} %get-tuple-element.11, bf16[384,1024]{1,0:T(8,128)(2,1)S(1)} %get-tuple-element.13, bf16[384,1024]{1,0:T(8,128)(2,1)S(1)} %get-tuple-element.14, ...), kind=kLoop, calls=%fused_computation.3 | loop fusion | flops 14680064 | bytes 13172736 | tf_op jit(solution)/shard_map/convert_element_type | solution.py:246
  (156 shorter events, 29.9 us)
Async XLA Ops:
  0.6 46.8 %copy-start = (bf16[1024,1024]{1,0:T(8,128)(2,1)S(1)}, bf16[1024,1024]{1,0:T(8,128)(2,1)}, u32[]{:S(2)}) copy-start(bf16[1024,1024]{1,0:T(8,128)(2,1)} %param.27) | copy-start | bytes 6291460
  2.5 29.6 %collective-permute-start = (bf16[64,1024]{1,0:T(8,128)(2,1)S(1)}, bf16[64,1024]{1,0:T(8,128)(2,1)S(1)}, u32[]{:S(2)}, u32[]{:S(2)}) collective-permute-start(bf16[64,1024]{1,0:T(8,128)(2,1)S(1)} %constant_dynamic-update-slice_fusion.4), channel_id=1, source_target_pairs={{0,8},{8,16},{16,24},{24,0},{1,9},{9,17},{17,25},{25,1},{2,10},{10... | collective-permute-start | bytes 393224 | tf_op jit(solution)/shard_map/ppermute | solution.py:166
  5.5 27.3 %collective-permute-start.1 = (bf16[64,1024]{1,0:T(8,128)(2,1)S(1)}, bf16[64,1024]{1,0:T(8,128)(2,1)S(1)}, u32[]{:S(2)}, u32[]{:S(2)}) collective-permute-start(bf16[64,1024]{1,0:T(8,128)(2,1)S(1)} %constant_dynamic-update-slice_fusion.4), channel_id=1, source_target_pairs={{0,16},{8,24},{16,0},{24,8},{1,17},{9,25},{17,1},{25,9},{2,18},{10... | collective-permute-start | bytes 393224 | tf_op jit(solution)/shard_map/ppermute | solution.py:166
  8.1 25.3 %collective-permute-start.2 = (bf16[64,1024]{1,0:T(8,128)(2,1)S(1)}, bf16[64,1024]{1,0:T(8,128)(2,1)S(1)}, u32[]{:S(2)}, u32[]{:S(2)}) collective-permute-start(bf16[64,1024]{1,0:T(8,128)(2,1)S(1)} %constant_dynamic-update-slice_fusion.4), channel_id=1, source_target_pairs={{0,24},{8,0},{16,8},{24,16},{1,25},{9,1},{17,9},{25,17},{2,26},{10... | collective-permute-start | bytes 393224 | tf_op jit(solution)/shard_map/ppermute | solution.py:166
  12.2 13.5 %copy-start.7 = (s32[512]{0:T(512)S(1)}, s32[512]{0:T(512)}, u32[]{:S(2)}) copy-start(s32[512]{0:T(512)} %param.19) | copy-start | bytes 6148
  24.6 5.9 %copy-start.8 = (s32[512,10]{0,1:T(8,128)S(1)}, s32[512,10]{0,1:T(8,128)}, u32[]{:S(2)}) copy-start(s32[512,10]{0,1:T(8,128)} %param.23) | copy-start | bytes 61444
  24.6 6.0 %copy-start.9 = (s32[512]{0:T(512)S(1)}, s32[512]{0:T(512)}, u32[]{:S(2)}) copy-start(s32[512]{0:T(512)} %param.25) | copy-start | bytes 6148
  27.6 11.2 %all-to-all-start = ((bf16[32,2,1024]{2,1,0:T(2,128)(2,1)}), bf16[32,2,1024]{2,1,0:T(2,128)(2,1)S(1)}, u32[]{:S(2)}, u32[]{:S(2)}) async-start(bf16[32,2,1024]{2,1,0:T(2,128)(2,1)} %reshape.56), calls=%async_computation | async-start | bytes 262144 | tf_op jit(solution)/shard_map/all_to_all | solution.py:182
  31.4 8.7 %copy-start.12 = (f32[1024]{0:T(1024)S(1)}, f32[1024]{0:T(1024)}, u32[]{:S(2)}) copy-start(f32[1024]{0:T(1024)} %param.22) | copy-start | bytes 12292
  39.7 2.4 %copy-start.10 = (s32[512]{0:T(512)S(1)}, s32[512]{0:T(512)}, u32[]{:S(2)}) copy-start(s32[512]{0:T(512)} %param.24) | copy-start | bytes 6148
  40.1 2.5 %copy-start.11 = (bf16[1024,1024]{1,0:T(8,128)(2,1)S(1)}, bf16[1024,1024]{1,0:T(8,128)(2,1)}, u32[]{:S(2)}) copy-start(bf16[1024,1024]{1,0:T(8,128)(2,1)} %param.26) | copy-start | bytes 6291460
  43.9 3.6 %copy-start.13 = (f32[1024]{0:T(1024)S(1)}, f32[1024]{0:T(1024)}, u32[]{:S(2)}) copy-start(f32[1024]{0:T(1024)} %param.28) | copy-start | bytes 12292
  47.5 2.6 %copy-start.14 = (bf16[512,1024]{1,0:T(8,128)(2,1)}, bf16[512,1024]{1,0:T(8,128)(2,1)S(1)}, u32[]{:S(2)}) copy-start(bf16[512,1024]{1,0:T(8,128)(2,1)S(1)} %divide_convert_fusion.1) | copy-start | bytes 3145732
  47.5 2.6 %copy-start.4 = (bf16[512,1024]{1,0:T(8,128)(2,1)S(1)}, bf16[512,1024]{1,0:T(8,128)(2,1)}, u32[]{:S(2)}) copy-start(bf16[512,1024]{1,0:T(8,128)(2,1)} %param.29) | copy-start | bytes 3145732
  61.7 7.5 %copy-start.2 = (bf16[768,1024]{1,0:T(8,128)(2,1)}, bf16[768,1024]{1,0:T(8,128)(2,1)S(1)}, u32[]{:S(2)}) copy-start(bf16[768,1024]{1,0:T(8,128)(2,1)S(1)} %get-tuple-element.10) | copy-start | bytes 4718596
  67.0 2.5 %copy-start.6 = (bf16[256,1024]{1,0:T(8,128)(2,1)S(1)}, bf16[256,1024]{1,0:T(8,128)(2,1)}, u32[]{:S(2)}) copy-start(bf16[256,1024]{1,0:T(8,128)(2,1)} %get-tuple-element.70) | copy-start | bytes 1572868
  67.0 2.8 %copy-start.3 = (bf16[512,1024]{1,0:T(8,128)(2,1)S(1)}, bf16[512,1024]{1,0:T(8,128)(2,1)}, u32[]{:S(2)}) copy-start(bf16[512,1024]{1,0:T(8,128)(2,1)} %slice.95) | copy-start | bytes 3145732
  68.0 3.1 %collective-permute-start.13 = (bf16[384,1024]{1,0:T(8,128)(2,1)}, bf16[384,1024]{1,0:T(8,128)(2,1)}, u32[]{:S(2)}, u32[]{:S(2)}) collective-permute-start(bf16[384,1024]{1,0:T(8,128)(2,1)} %constant_dynamic-slice_fusion.9), channel_id=1, source_target_pairs={{0,1},{1,0},{2,3},{3,2},{4,5},{5,4},{6,7},{7,6},{8,9},{9,8},{10,11... | collective-permute-start | bytes 2359304 | tf_op jit(solution)/shard_map/ppermute | solution.py:26
  69.2 4.2 %collective-permute-start.3 = (bf16[384,1024]{1,0:T(8,128)(2,1)}, bf16[384,1024]{1,0:T(8,128)(2,1)}, u32[]{:S(2)}, u32[]{:S(2)}) collective-permute-start(bf16[384,1024]{1,0:T(8,128)(2,1)} %constant_dynamic-slice_fusion.14), channel_id=1, source_target_pairs={{0,1},{1,0},{2,3},{3,2},{4,5},{5,4},{6,7},{7,6},{8,9},{9,8},{10,11... | collective-permute-start | bytes 2359304 | tf_op jit(solution)/shard_map/ppermute | solution.py:26
  70.9 4.8 %collective-permute-start.23 = (bf16[400,1024]{1,0:T(8,128)(2,1)}, bf16[400,1024]{1,0:T(8,128)(2,1)}, u32[]{:S(2)}, u32[]{:S(2)}) collective-permute-start(bf16[400,1024]{1,0:T(8,128)(2,1)} %constant_dynamic-slice_fusion.4), channel_id=1, source_target_pairs={{0,1},{1,0},{2,3},{3,2},{4,5},{5,4},{6,7},{7,6},{8,9},{9,8},{10,11... | collective-permute-start | bytes 2457608 | tf_op jit(solution)/shard_map/ppermute | solution.py:26
  72.9 11.4 %collective-permute-start.14 = (bf16[192,1024]{1,0:T(8,128)(2,1)S(1)}, bf16[192,1024]{1,0:T(8,128)(2,1)S(1)}, u32[]{:S(2)}, u32[]{:S(2)}) collective-permute-start(bf16[192,1024]{1,0:T(8,128)(2,1)S(1)} %constant_dynamic-slice_fusion.8), channel_id=1, source_target_pairs={{0,4},{1,5},{2,6},{3,7},{4,0},{5,1},{6,2},{7,3},{8,12},{9,13},{10,... | collective-permute-start | bytes 1179656 | tf_op jit(solution)/shard_map/ppermute | solution.py:26
  74.9 11.3 %collective-permute-start.4 = (bf16[192,1024]{1,0:T(8,128)(2,1)S(1)}, bf16[192,1024]{1,0:T(8,128)(2,1)S(1)}, u32[]{:S(2)}, u32[]{:S(2)}) collective-permute-start(bf16[192,1024]{1,0:T(8,128)(2,1)S(1)} %constant_dynamic-slice_fusion.13), channel_id=1, source_target_pairs={{0,2},{1,3},{2,0},{3,1},{4,6},{5,7},{6,4},{7,5},{8,10},{9,11},{10,... | collective-permute-start | bytes 1179656 | tf_op jit(solution)/shard_map/ppermute | solution.py:26
  77.2 12.4 %collective-permute-start.24 = (bf16[200,1024]{1,0:T(8,128)(2,1)S(1)}, bf16[200,1024]{1,0:T(8,128)(2,1)S(1)}, u32[]{:S(2)}, u32[]{:S(2)}) collective-permute-start(bf16[200,1024]{1,0:T(8,128)(2,1)S(1)} %constant_dynamic-slice_fusion.3), channel_id=1, source_target_pairs={{0,8},{8,0},{16,24},{24,16},{1,9},{9,1},{17,25},{25,17},{2,10},{10... | collective-permute-start | bytes 1228808 | tf_op jit(solution)/shard_map/ppermute | solution.py:26
  84.4 9.8 %collective-permute-start.15 = (bf16[96,1024]{1,0:T(8,128)(2,1)S(1)}, bf16[96,1024]{1,0:T(8,128)(2,1)S(1)}, u32[]{:S(2)}, u32[]{:S(2)}) collective-permute-start(bf16[96,1024]{1,0:T(8,128)(2,1)S(1)} %constant_dynamic-slice_fusion.7), channel_id=1, source_target_pairs={{0,8},{8,0},{16,24},{24,16},{1,9},{9,1},{17,25},{25,17},{2,10},{10... | collective-permute-start | bytes 589832 | tf_op jit(solution)/shard_map/ppermute | solution.py:26
  86.3 8.6 %collective-permute-start.5 = (bf16[96,1024]{1,0:T(8,128)(2,1)S(1)}, bf16[96,1024]{1,0:T(8,128)(2,1)S(1)}, u32[]{:S(2)}, u32[]{:S(2)}) collective-permute-start(bf16[96,1024]{1,0:T(8,128)(2,1)S(1)} %constant_dynamic-slice_fusion.12), channel_id=1, source_target_pairs={{0,4},{1,5},{2,6},{3,7},{4,0},{5,1},{6,2},{7,3},{8,12},{9,13},{10,... | collective-permute-start | bytes 589832 | tf_op jit(solution)/shard_map/ppermute | solution.py:26
  89.8 14.0 %collective-permute-start.25 = (bf16[100,1024]{1,0:T(8,128)(2,1)S(1)}, bf16[100,1024]{1,0:T(8,128)(2,1)S(1)}, u32[]{:S(2)}, u32[]{:S(2)}) collective-permute-start(bf16[100,1024]{1,0:T(8,128)(2,1)S(1)} %constant_dynamic-slice_fusion.2), channel_id=1, source_target_pairs={{0,16},{8,24},{16,0},{24,8},{1,17},{9,25},{17,1},{25,9},{2,18},{10... | collective-permute-start | bytes 614408 | tf_op jit(solution)/shard_map/ppermute | solution.py:26
  94.3 10.9 %collective-permute-start.16 = (bf16[48,1024]{1,0:T(8,128)(2,1)S(1)}, bf16[48,1024]{1,0:T(8,128)(2,1)S(1)}, u32[]{:S(2)}, u32[]{:S(2)}) collective-permute-start(bf16[48,1024]{1,0:T(8,128)(2,1)S(1)} %constant_dynamic-slice_fusion.6), channel_id=1, source_target_pairs={{0,16},{8,24},{16,0},{24,8},{1,17},{9,25},{17,1},{25,9},{2,18},{10... | collective-permute-start | bytes 294920 | tf_op jit(solution)/shard_map/ppermute | solution.py:26
  95.1 11.4 %collective-permute-start.6 = (bf16[48,1024]{1,0:T(8,128)(2,1)S(1)}, bf16[48,1024]{1,0:T(8,128)(2,1)S(1)}, u32[]{:S(2)}, u32[]{:S(2)}) collective-permute-start(bf16[48,1024]{1,0:T(8,128)(2,1)S(1)} %constant_dynamic-slice_fusion.11), channel_id=1, source_target_pairs={{0,8},{8,0},{16,24},{24,16},{1,9},{9,1},{17,25},{25,17},{2,10},{10... | collective-permute-start | bytes 294920 | tf_op jit(solution)/shard_map/ppermute | solution.py:26
  104.0 8.2 %collective-permute-start.26 = (bf16[50,1024]{1,0:T(8,128)(2,1)S(1)}, bf16[50,1024]{1,0:T(8,128)(2,1)S(1)}, u32[]{:S(2)}, u32[]{:S(2)}) collective-permute-start(bf16[50,1024]{1,0:T(8,128)(2,1)S(1)} %constant_dynamic-slice_fusion.1), channel_id=1, source_target_pairs={{0,2},{1,3},{2,0},{3,1},{4,6},{5,7},{6,4},{7,5},{8,10},{9,11},{10,... | collective-permute-start | bytes 307208 | tf_op jit(solution)/shard_map/ppermute | solution.py:26
  105.2 4.6 %collective-permute-start.17 = (bf16[24,1024]{1,0:T(8,128)(2,1)S(1)}, bf16[24,1024]{1,0:T(8,128)(2,1)S(1)}, u32[]{:S(2)}, u32[]{:S(2)}) collective-permute-start(bf16[24,1024]{1,0:T(8,128)(2,1)S(1)} %constant_dynamic-slice_fusion.5), channel_id=1, source_target_pairs={{0,2},{1,3},{2,0},{3,1},{4,6},{5,7},{6,4},{7,5},{8,10},{9,11},{10,... | collective-permute-start | bytes 147464 | tf_op jit(solution)/shard_map/ppermute | solution.py:26
  106.5 5.6 %collective-permute-start.7 = (bf16[24,1024]{1,0:T(8,128)(2,1)S(1)}, bf16[24,1024]{1,0:T(8,128)(2,1)S(1)}, u32[]{:S(2)}, u32[]{:S(2)}) collective-permute-start(bf16[24,1024]{1,0:T(8,128)(2,1)S(1)} %constant_dynamic-slice_fusion.10), channel_id=1, source_target_pairs={{0,16},{8,24},{16,0},{24,8},{1,17},{9,25},{17,1},{25,9},{2,18},{10... | collective-permute-start | bytes 147464 | tf_op jit(solution)/shard_map/ppermute | solution.py:26
  109.9 4.2 %collective-permute-start.18 = (bf16[24,1024]{1,0:T(8,128)(2,1)S(1)}, bf16[24,1024]{1,0:T(8,128)(2,1)S(1)}, u32[]{:S(2)}, u32[]{:S(2)}) collective-permute-start(bf16[24,1024]{1,0:T(8,128)(2,1)S(1)} %add_convert_fusion.14), channel_id=1, source_target_pairs={{0,2},{1,3},{2,0},{3,1},{4,6},{5,7},{6,4},{7,5},{8,10},{9,11},{10,... | collective-permute-start | bytes 147464 | tf_op jit(solution)/shard_map/ppermute | solution.py:26
  112.1 5.1 %collective-permute-start.8 = (bf16[24,1024]{1,0:T(8,128)(2,1)S(1)}, bf16[24,1024]{1,0:T(8,128)(2,1)S(1)}, u32[]{:S(2)}, u32[]{:S(2)}) collective-permute-start(bf16[24,1024]{1,0:T(8,128)(2,1)S(1)} %add_convert_fusion.15), channel_id=1, source_target_pairs={{0,16},{8,24},{16,0},{24,8},{1,17},{9,25},{17,1},{25,9},{2,18},{10... | collective-permute-start | bytes 147464 | tf_op jit(solution)/shard_map/ppermute | solution.py:26
  112.2 4.9 %collective-permute-start.27 = (bf16[25,1024]{1,0:T(8,128)(2,1)S(1)}, bf16[25,1024]{1,0:T(8,128)(2,1)S(1)}, u32[]{:S(2)}, u32[]{:S(2)}) collective-permute-start(bf16[25,1024]{1,0:T(8,128)(2,1)S(1)} %constant_dynamic-slice_fusion), channel_id=1, source_target_pairs={{0,4},{1,5},{2,6},{3,7},{4,0},{5,1},{6,2},{7,3},{8,12},{9,13},{10,... | collective-permute-start | bytes 153608 | tf_op jit(solution)/shard_map/ppermute | solution.py:26
  114.1 9.1 %collective-permute-start.19 = (bf16[48,1024]{1,0:T(8,128)(2,1)S(1)}, bf16[48,1024]{1,0:T(8,128)(2,1)S(1)}, u32[]{:S(2)}, u32[]{:S(2)}) collective-permute-start(bf16[48,1024]{1,0:T(8,128)(2,1)S(1)} %pad_maximum_fusion.17), channel_id=1, source_target_pairs={{0,16},{8,24},{16,0},{24,8},{1,17},{9,25},{17,1},{25,9},{2,18},{10... | collective-permute-start | bytes 294920 | tf_op jit(solution)/shard_map/ppermute | solution.py:26
  117.2 5.0 %collective-permute-start.28 = (bf16[25,1024]{1,0:T(8,128)(2,1)S(1)}, bf16[25,1024]{1,0:T(8,128)(2,1)S(1)}, u32[]{:S(2)}, u32[]{:S(2)}) collective-permute-start(bf16[25,1024]{1,0:T(8,128)(2,1)S(1)} %add_convert_fusion.13), channel_id=1, source_target_pairs={{0,4},{1,5},{2,6},{3,7},{4,0},{5,1},{6,2},{7,3},{8,12},{9,13},{10,... | collective-permute-start | bytes 153608 | tf_op jit(solution)/shard_map/ppermute | solution.py:26
  118.5 6.2 %collective-permute-start.9 = (bf16[48,1024]{1,0:T(8,128)(2,1)S(1)}, bf16[48,1024]{1,0:T(8,128)(2,1)S(1)}, u32[]{:S(2)}, u32[]{:S(2)}) collective-permute-start(bf16[48,1024]{1,0:T(8,128)(2,1)S(1)} %pad_maximum_fusion.16), channel_id=1, source_target_pairs={{0,8},{8,0},{16,24},{24,16},{1,9},{9,1},{17,25},{25,17},{2,10},{10... | collective-permute-start | bytes 294920 | tf_op jit(solution)/shard_map/ppermute | solution.py:26
  122.3 6.1 %collective-permute-start.29 = (bf16[50,1024]{1,0:T(8,128)(2,1)S(1)}, bf16[50,1024]{1,0:T(8,128)(2,1)S(1)}, u32[]{:S(2)}, u32[]{:S(2)}) collective-permute-start(bf16[50,1024]{1,0:T(8,128)(2,1)S(1)} %pad_maximum_fusion.15), channel_id=1, source_target_pairs={{0,2},{1,3},{2,0},{3,1},{4,6},{5,7},{6,4},{7,5},{8,10},{9,11},{10,... | collective-permute-start | bytes 307208 | tf_op jit(solution)/shard_map/ppermute | solution.py:26
  123.3 7.6 %collective-permute-start.20 = (bf16[96,1024]{1,0:T(8,128)(2,1)S(1)}, bf16[96,1024]{1,0:T(8,128)(2,1)S(1)}, u32[]{:S(2)}, u32[]{:S(2)}) collective-permute-start(bf16[96,1024]{1,0:T(8,128)(2,1)S(1)} %pad_maximum_fusion.14), channel_id=1, source_target_pairs={{0,8},{8,0},{16,24},{24,16},{1,9},{9,1},{17,25},{25,17},{2,10},{10... | collective-permute-start | bytes 589832 | tf_op jit(solution)/shard_map/ppermute | solution.py:26
  124.8 7.4 %collective-permute-start.10 = (bf16[96,1024]{1,0:T(8,128)(2,1)S(1)}, bf16[96,1024]{1,0:T(8,128)(2,1)S(1)}, u32[]{:S(2)}, u32[]{:S(2)}) collective-permute-start(bf16[96,1024]{1,0:T(8,128)(2,1)S(1)} %pad_maximum_fusion.13), channel_id=1, source_target_pairs={{0,4},{1,5},{2,6},{3,7},{4,0},{5,1},{6,2},{7,3},{8,12},{9,13},{10,... | collective-permute-start | bytes 589832 | tf_op jit(solution)/shard_map/ppermute | solution.py:26
  128.4 9.0 %collective-permute-start.30 = (bf16[100,1024]{1,0:T(8,128)(2,1)S(1)}, bf16[100,1024]{1,0:T(8,128)(2,1)S(1)}, u32[]{:S(2)}, u32[]{:S(2)}) collective-permute-start(bf16[100,1024]{1,0:T(8,128)(2,1)S(1)} %pad_maximum_fusion.12), channel_id=1, source_target_pairs={{0,16},{8,24},{16,0},{24,8},{1,17},{9,25},{17,1},{25,9},{2,18},{10... | collective-permute-start | bytes 614408 | tf_op jit(solution)/shard_map/ppermute | solution.py:26
  130.9 7.8 %collective-permute-start.21 = (bf16[192,1024]{1,0:T(8,128)(2,1)S(1)}, bf16[192,1024]{1,0:T(8,128)(2,1)S(1)}, u32[]{:S(2)}, u32[]{:S(2)}) collective-permute-start(bf16[192,1024]{1,0:T(8,128)(2,1)S(1)} %pad_maximum_fusion.11), channel_id=1, source_target_pairs={{0,4},{1,5},{2,6},{3,7},{4,0},{5,1},{6,2},{7,3},{8,12},{9,13},{10,... | collective-permute-start | bytes 1179656 | tf_op jit(solution)/shard_map/ppermute | solution.py:26
  132.3 7.8 %collective-permute-start.11 = (bf16[192,1024]{1,0:T(8,128)(2,1)S(1)}, bf16[192,1024]{1,0:T(8,128)(2,1)S(1)}, u32[]{:S(2)}, u32[]{:S(2)}) collective-permute-start(bf16[192,1024]{1,0:T(8,128)(2,1)S(1)} %pad_maximum_fusion.10), channel_id=1, source_target_pairs={{0,2},{1,3},{2,0},{3,1},{4,6},{5,7},{6,4},{7,5},{8,10},{9,11},{10,... | collective-permute-start | bytes 1179656 | tf_op jit(solution)/shard_map/ppermute | solution.py:26
  137.6 8.0 %collective-permute-start.31 = (bf16[200,1024]{1,0:T(8,128)(2,1)S(1)}, bf16[200,1024]{1,0:T(8,128)(2,1)S(1)}, u32[]{:S(2)}, u32[]{:S(2)}) collective-permute-start(bf16[200,1024]{1,0:T(8,128)(2,1)S(1)} %pad_maximum_fusion.9), channel_id=1, source_target_pairs={{0,8},{8,0},{16,24},{24,16},{1,9},{9,1},{17,25},{25,17},{2,10},{10... | collective-permute-start | bytes 1228808 | tf_op jit(solution)/shard_map/ppermute | solution.py:26
  139.9 6.9 %collective-permute-start.22 = (bf16[384,1024]{1,0:T(8,128)(2,1)}, bf16[384,1024]{1,0:T(8,128)(2,1)}, u32[]{:S(2)}, u32[]{:S(2)}) collective-permute-start(bf16[384,1024]{1,0:T(8,128)(2,1)} %pad_maximum_fusion.8), channel_id=1, source_target_pairs={{0,1},{1,0},{2,3},{3,2},{4,5},{5,4},{6,7},{7,6},{8,9},{9,8},{10,11... | collective-permute-start | bytes 2359304 | tf_op jit(solution)/shard_map/ppermute | solution.py:26
  141.3 7.1 %collective-permute-start.12 = (bf16[384,1024]{1,0:T(8,128)(2,1)}, bf16[384,1024]{1,0:T(8,128)(2,1)}, u32[]{:S(2)}, u32[]{:S(2)}) collective-permute-start(bf16[384,1024]{1,0:T(8,128)(2,1)} %pad_maximum_fusion.7), channel_id=1, source_target_pairs={{0,1},{1,0},{2,3},{3,2},{4,5},{5,4},{6,7},{7,6},{8,9},{9,8},{10,11... | collective-permute-start | bytes 2359304 | tf_op jit(solution)/shard_map/ppermute | solution.py:26
  146.8 3.1 %collective-permute-start.32 = (bf16[400,1024]{1,0:T(8,128)(2,1)}, bf16[400,1024]{1,0:T(8,128)(2,1)S(1)}, u32[]{:S(2)}, u32[]{:S(2)}) collective-permute-start(bf16[400,1024]{1,0:T(8,128)(2,1)} %pad_maximum_fusion.6), channel_id=1, source_target_pairs={{0,1},{1,0},{2,3},{3,2},{4,5},{5,4},{6,7},{7,6},{8,9},{9,8},{10,11... | collective-permute-start | bytes 2457608 | tf_op jit(solution)/shard_map/ppermute | solution.py:26
  151.8 3.8 %copy-start.1 = (bf16[1024,1024]{1,0:T(8,128)(2,1)S(1)}, bf16[1024,1024]{1,0:T(8,128)(2,1)}, u32[]{:S(2)}) copy-start(bf16[1024,1024]{1,0:T(8,128)(2,1)} %param.27) | copy-start | bytes 6291460
  (1 other events, 1.8 us)
